TPU v7x, 32 devices: a whole 2x2x4 slice. The times are simulated.
32 devices in a mesh: dp: 4 (over y, x), tensor: 8 (over z, core).
Axes of the slice: x: 2, y: 2, z: 4, core: 2. Of those that a mesh axis runs over, the one named last changes fastest.
Arguments:
- prompt_states: bfloat16 [8, 512, 2048], P('dp', 'tensor')
- decode_states: bfloat16 [128, 2048], P(('dp', 'tensor'))
- cache: bfloat16 [2, 136, 384, 2048], P(None, 'dp', 'tensor'), may hold values from -160 to 160
- prompt_starts: int32 [8], replicated, may hold values from 0 to 384, as said below
- decode_lengths: int32 [128], replicated, may hold values from 1 to 384, as said below
- decode_slots: int32 [128], replicated, may hold values from 0 to 127, each once
- w_qkv: bfloat16 [3, 2048, 2048], P(None, None, 'tensor')
- w_out: bfloat16 [2048, 2048], P('tensor')
- w_gate_up: bfloat16 [2, 2048, 8192], P(None, None, 'tensor')
- w_down: bfloat16 [8192, 2048], P('tensor')
- gains: float32 [4, 2048], replicated, may hold values from 0.25 to 1.75
Outputs:
- prompt_out: bfloat16 [8, 512, 2048], P('dp', 'tensor')
- decode_out: bfloat16 [128, 2048], P(('dp', 'tensor'))
- new_prompt_kv: bfloat16 [2, 8, 512, 2048], P(None, 'dp', 'tensor')
- new_decode_kv: bfloat16 [2, 128, 2048], P(None, ('dp', 'tensor'))
Inputs may be any that keep to these rules, and one draw needn't show every extreme that they name: Decode request e sits in decode slot decode_slots[e]; each slot holds one request. `prompt_starts`: some prompt has exactly 384 cached positions. `decode_lengths`: some decode request has exactly 384 cached positions.
All inputs are finite; a program needn't handle non-finite values.
Results may differ from a plain program's by a relative error of at most 0.02.
Values may be sent and summed in bfloat16 or wider, within the bound.
No kernel may reach another device: no remote copies, remote signals or barrier semaphores. Data moves between devices by JAX's collectives and lax.ppermute only.
A program may use at most 256 MiB of HBM per device.

v0:
```python
import jax
import jax.numpy as jnp
from jax import lax
from jax.sharding import PartitionSpec as P

HD = 128


EPSILON = 1e-06
ROPE_BASE = 500000.0
MASKED_SCORE = -1e30


def rms_scale(values, gain_vec):
    return (
        values * lax.rsqrt(jnp.mean(values * values, axis=-1, keepdims=True) + EPSILON) * gain_vec
    )


def rotate(values, positions):
    full_shape = values.shape
    paired = values.reshape(full_shape[:-1] + (full_shape[-1] // HD, HD // 2, 2))
    freq_index = jnp.arange(HD // 2, dtype=jnp.float32)
    inv_freq = jnp.power(ROPE_BASE, -2.0 * freq_index / HD)
    angles = positions.astype(jnp.float32)[..., None, None] * inv_freq
    cosine = jnp.cos(angles)
    sine_values = jnp.sin(angles)
    even_part = paired[..., 0]
    odd_part = paired[..., 1]
    turned = jnp.stack(
        [even_part * cosine - odd_part * sine_values, even_part * sine_values + odd_part * cosine],
        axis=-1,
    )
    return turned.reshape(full_shape)


def split_rows(stacked, tensors, pre_dev, part_rows):
    tail_shape = stacked.shape[1:]
    per_device = stacked.shape[0] // tensors
    device_grid = stacked.reshape((tensors, per_device) + tail_shape)
    prompt_part = device_grid[:, : pre_dev * part_rows].reshape(
        (tensors, pre_dev, part_rows) + tail_shape
    )
    prompt_part = jnp.swapaxes(prompt_part, 0, 1).reshape(
        (pre_dev, tensors * part_rows) + tail_shape
    )
    decode_part = device_grid[:, pre_dev * part_rows :].reshape((-1,) + tail_shape)
    return (prompt_part, decode_part)


def join_rows(prompt_part, decode_part, tensors):
    pre_dev = prompt_part.shape[0]
    part_rows = prompt_part.shape[1] // tensors
    tail_shape = prompt_part.shape[2:]
    leading = jnp.swapaxes(prompt_part.reshape((pre_dev, tensors, part_rows) + tail_shape), 0, 1)
    leading = leading.reshape((tensors, pre_dev * part_rows) + tail_shape)
    trailing = decode_part.reshape((tensors, -1) + tail_shape)
    return jnp.concatenate([leading, trailing], axis=1).reshape((-1,) + tail_shape)


def spread(local_rows, weights):
    return jnp.einsum(
        "rd,kdc->rkc",
        lax.all_gather(local_rows, "tensor", axis=0, tiled=True),
        weights,
        preferred_element_type=jnp.float32,
    )


def collect(operand, weights):
    return lax.psum_scatter(
        jnp.dot(operand, weights, preferred_element_type=jnp.float32).astype(jnp.bfloat16),
        "tensor",
        scatter_dimension=0,
        tiled=True,
    ).astype(jnp.float32)


def local(
    prompt_states,
    decode_states,
    cache,
    prompt_starts,
    decode_lengths,
    decode_slots,
    w_qkv,
    w_out,
    w_gate_up,
    w_down,
    gains,
):
    tensors = lax.axis_size("tensor")
    tensor_pos = lax.axis_index("tensor")
    data_pos = lax.axis_index("dp")
    pre_dev, part_rows, model_width = prompt_states.shape
    dec_part = decode_states.shape[0]
    group_len = part_rows * tensors
    dec_dev = dec_part * tensors
    ctx_part = cache.shape[2]
    head_count = model_width // HD
    prompt_own = pre_dev * part_rows
    own_rows = prompt_own + dec_part
    states = jnp.concatenate(
        [prompt_states.reshape(prompt_own, model_width), decode_states], axis=0
    )
    starts = lax.dynamic_slice_in_dim(prompt_starts, data_pos * pre_dev, pre_dev)
    slot_ids = data_pos * dec_dev + jnp.arange(dec_dev, dtype=jnp.int32)
    matches = decode_slots[None, :] == slot_ids[:, None]
    slot_length = jnp.sum(jnp.where(matches, decode_lengths[None, :], 0), axis=1)
    offsets = jnp.arange(group_len, dtype=jnp.int32)
    prompt_pos = starts[:, None] + offsets[None, :]
    own_prompt_pos = lax.dynamic_slice_in_dim(
        prompt_pos, tensor_pos * part_rows, part_rows, 1
    ).reshape(prompt_own)
    own_decode_pos = lax.dynamic_slice_in_dim(slot_length, tensor_pos * dec_part, dec_part)
    own_pos = jnp.concatenate([own_prompt_pos, own_decode_pos], axis=0)
    projected = spread(states, w_qkv)
    query_raw = projected[:, 0].astype(jnp.bfloat16)
    key_raw = projected[:, 1].astype(jnp.bfloat16)
    value_raw = projected[:, 2].astype(jnp.bfloat16)
    query_all, key_all, value_all = (
        lax.all_gather(query_raw, "tensor", axis=1, tiled=True),
        lax.all_gather(key_raw, "tensor", axis=1, tiled=True),
        lax.all_gather(value_raw, "tensor", axis=1, tiled=True),
    )
    key_own = lax.dynamic_slice_in_dim(key_all, tensor_pos * own_rows, own_rows, 0)
    value_own = lax.dynamic_slice_in_dim(value_all, tensor_pos * own_rows, own_rows, 0)
    query_prompt, query_decode = split_rows(query_all, tensors, pre_dev, part_rows)
    query_prompt = rotate(rms_scale(query_prompt.astype(jnp.float32), gains[0]), prompt_pos).astype(
        jnp.bfloat16
    )
    query_decode = rotate(
        rms_scale(query_decode.astype(jnp.float32), gains[0]), slot_length
    ).astype(jnp.bfloat16)
    key_new = rotate(rms_scale(key_own.astype(jnp.float32), gains[1]), own_pos).astype(jnp.bfloat16)
    scale_factor = HD ** (-0.5)
    cache_pos = tensor_pos * ctx_part + jnp.arange(ctx_part, dtype=jnp.int32)
    prompt_q = query_prompt.reshape(pre_dev, group_len, head_count, HD)
    prompt_keys = cache[0, :pre_dev].reshape(pre_dev, ctx_part, head_count, HD)
    prompt_values = cache[1, :pre_dev].reshape(pre_dev, ctx_part, head_count, HD)
    fresh_keys = key_new[:prompt_own].reshape(pre_dev, part_rows, head_count, HD)
    fresh_values = value_own[:prompt_own].reshape(pre_dev, part_rows, head_count, HD)
    cached_scores = jnp.einsum(
        "aihe,ajhe->ahij", prompt_q, prompt_keys, preferred_element_type=jnp.float32
    )
    fresh_scores = jnp.einsum(
        "aihe,ajhe->ahij", prompt_q, fresh_keys, preferred_element_type=jnp.float32
    )
    prompt_scores = jnp.concatenate([cached_scores, fresh_scores], axis=-1) * scale_factor
    key_offsets = tensor_pos * part_rows + jnp.arange(part_rows, dtype=jnp.int32)
    live_cached = jnp.broadcast_to(
        (cache_pos[None, :] < starts[:, None])[:, None, None, :], (pre_dev, 1, group_len, ctx_part)
    )
    live_fresh = jnp.broadcast_to(
        (key_offsets[None, :] <= offsets[:, None])[None, None], (pre_dev, 1, group_len, part_rows)
    )
    prompt_live = jnp.concatenate([live_cached, live_fresh], axis=-1)
    prompt_masked = jnp.where(prompt_live, prompt_scores, MASKED_SCORE)
    prompt_top = jnp.max(prompt_masked, axis=-1)
    decode_q = query_decode.reshape(dec_dev, head_count, HD)
    decode_keys = cache[0, pre_dev:].reshape(dec_dev, ctx_part, head_count, HD)
    decode_values = cache[1, pre_dev:].reshape(dec_dev, ctx_part, head_count, HD)
    own_keys = key_new[prompt_own:].reshape(dec_part, head_count, HD)
    own_values = value_own[prompt_own:].reshape(dec_part, head_count, HD)
    decode_cached = jnp.einsum(
        "she,sjhe->shj", decode_q, decode_keys, preferred_element_type=jnp.float32
    )
    decode_fresh = jnp.einsum(
        "she,jhe->shj", decode_q, own_keys, preferred_element_type=jnp.float32
    )
    decode_scores = jnp.concatenate([decode_cached, decode_fresh], axis=-1) * scale_factor
    live_slots = (cache_pos[None, :] < slot_length[:, None])[:, None, :]
    own_ids = tensor_pos * dec_part + jnp.arange(dec_part, dtype=jnp.int32)
    live_owned = (jnp.arange(dec_dev, dtype=jnp.int32)[:, None] == own_ids[None, :])[:, None, :]
    decode_live = jnp.concatenate([live_slots, live_owned], axis=-1)
    decode_masked = jnp.where(decode_live, decode_scores, MASKED_SCORE)
    decode_top = jnp.max(decode_masked, axis=-1)
    prompt_weights = jnp.where(prompt_live, jnp.exp(prompt_masked - prompt_top[..., None]), 0.0)
    prompt_total = jnp.sum(prompt_weights, axis=-1)
    prompt_probs = prompt_weights.astype(jnp.bfloat16)
    prompt_mixed = jnp.einsum(
        "ahij,ajhe->aihe",
        prompt_probs[..., :ctx_part],
        prompt_values,
        preferred_element_type=jnp.float32,
    )
    prompt_mixed = prompt_mixed + jnp.einsum(
        "ahij,ajhe->aihe",
        prompt_probs[..., ctx_part:],
        fresh_values,
        preferred_element_type=jnp.float32,
    )
    decode_weights = jnp.where(decode_live, jnp.exp(decode_masked - decode_top[..., None]), 0.0)
    decode_total = jnp.sum(decode_weights, axis=-1)
    decode_probs = decode_weights.astype(jnp.bfloat16)
    decode_mixed = jnp.einsum(
        "shj,sjhe->she",
        decode_probs[..., :ctx_part],
        decode_values,
        preferred_element_type=jnp.float32,
    )
    decode_mixed = decode_mixed + jnp.einsum(
        "shj,jhe->she", decode_probs[..., ctx_part:], own_values, preferred_element_type=jnp.float32
    )
    totals = join_rows(jnp.swapaxes(prompt_total, 1, 2), decode_total, tensors)
    mixed = join_rows(
        prompt_mixed.reshape(pre_dev, group_len, model_width),
        decode_mixed.reshape(dec_dev, model_width),
        tensors,
    )
    tops = join_rows(jnp.swapaxes(prompt_top, 1, 2), decode_top, tensors)
    got_tops, got_totals, got_mixed = (
        lax.all_to_all(tops, "tensor", split_axis=0, concat_axis=0, tiled=True),
        lax.all_to_all(totals, "tensor", split_axis=0, concat_axis=0, tiled=True),
        lax.all_to_all(mixed, "tensor", split_axis=0, concat_axis=0, tiled=True),
    )
    got_tops = got_tops.reshape(tensors, own_rows, head_count)
    got_totals = got_totals.reshape(tensors, own_rows, head_count)
    got_mixed = got_mixed.reshape(tensors, own_rows, head_count, HD)
    highest = jnp.max(got_tops, axis=0)
    factors = jnp.exp(got_tops - highest[None])
    total_all = jnp.sum(got_totals * factors, axis=0)
    shares = lax.optimization_barrier((got_mixed * factors[..., None]).astype(jnp.bfloat16))
    mixed_all = jnp.sum(shares.astype(jnp.float32), axis=0)
    attended_own = (
        (mixed_all / total_all[..., None]).reshape(own_rows, model_width).astype(jnp.bfloat16)
    )
    my_columns = lax.all_to_all(attended_own, "tensor", split_axis=1, concat_axis=0, tiled=True)
    attn_sum = collect(my_columns, w_out)
    hidden = (states.astype(jnp.float32) + rms_scale(attn_sum, gains[2])).astype(jnp.bfloat16)
    gate_up = spread(hidden, w_gate_up)
    activated = (jax.nn.silu(gate_up[:, 0]) * gate_up[:, 1]).astype(jnp.bfloat16)
    ffn_sum = collect(activated, w_down)
    output = (hidden.astype(jnp.float32) + rms_scale(ffn_sum, gains[3])).astype(jnp.bfloat16)
    prompt_out = output[:prompt_own].reshape(pre_dev, part_rows, model_width)
    everyone = lax.all_gather(output[prompt_own:], ("dp", "tensor"), axis=0, tiled=True)
    wanted = lax.dynamic_slice_in_dim(
        decode_slots, (data_pos * tensors + tensor_pos) * dec_part, dec_part
    )
    decode_out = jnp.take(everyone, wanted, axis=0)
    new_prompt_kv = jnp.stack([key_new[:prompt_own], value_own[:prompt_own]]).reshape(
        2, pre_dev, part_rows, model_width
    )
    new_decode_kv = jnp.stack([key_new[prompt_own:], value_own[prompt_own:]])
    return (prompt_out, decode_out, new_prompt_kv, new_decode_kv)


def solution(mesh):
    in_specs = (
        P("dp", "tensor", None),
        P(("dp", "tensor"), None),
        P(None, "dp", "tensor", None),
        P(),
        P(),
        P(),
        P(None, None, "tensor"),
        P("tensor", None),
        P(None, None, "tensor"),
        P("tensor", None),
        P(),
    )
    out_specs = (
        P("dp", "tensor", None),
        P(("dp", "tensor"), None),
        P(None, "dp", "tensor", None),
        P(None, ("dp", "tensor"), None),
    )
    return jax.shard_map(local, mesh=mesh, in_specs=in_specs, out_specs=out_specs, check_vma=False)
```

profile of v0, /device:TPU:0, one launch (start us, length us, event | category | flops | bytes accessed | tf_op | source)
XLA Modules:
  0.0 856.1 jit_solution(17984813382388195852)
XLA Ops:
  9.4 53.1 %all-gather.18.cloned.1.call-done = bf16[8,132,2048]{2,1,0:T(8,128)(2,1)} async-done(((bf16[1,132,2048]{2,1,0:T(8,128)(2,1)}), bf16[8,132,2048]{2,1,0:T(8,128)(2,1)}) %all-gather.18.cloned.1.call-update) | async-done | bytes 4325392 | tf_op jit(solution)/shard_map/all_gather | solution.py:64
  62.5 5.2 reshape.567
  67.7 5.8 convolution_convert_fusion.2
  78.6 6.0 fusion.48
  84.7 5.1 copy.168
  90.6 5.0 copy.169
  98.9 23.6 %all-gather.12.cloned.1.call-done = bf16[1056,1,2048]{2,0,1:T(8,128)(2,1)} async-done(((bf16[1056,1,256]{2,0,1:T(8,128)(2,1)}), bf16[1056,1,2048]{2,0,1:T(8,128)(2,1)}) %all-gather.12.cloned.1.call-update) | async-done | bytes 4325392 | tf_op jit(solution)/shard_map/all_gather | solution.py:122
  122.5 5.1 reshape.516
  127.7 6.8 slice_convert_fusion
  135.4 36.5 %all-gather.14.cloned.1.call-done = bf16[1056,1,2048]{2,0,1:T(8,128)(2,1)} async-done(((bf16[1056,1,256]{2,0,1:T(8,128)(2,1)}), bf16[1056,1,2048]{2,0,1:T(8,128)(2,1)}) %all-gather.14.cloned.1.call-update) | async-done | bytes 4325392 | tf_op jit(solution)/shard_map/all_gather | solution.py:123
  173.2 12.5 %copy.115 = f32[8,2,64,2048]{2,0,3,1:T(8,128)} copy(f32[8,2,64,2048]{3,2,1,0:T(8,128)} %bitcast.143) | data formatting | bytes 16777216 | tf_op jit(solution)/shard_map/convert_element_type | solution.py:129
  185.7 15.2 %reshape.531 = f32[2,512,16,64,2]{1,4,3,2,0:T(2,128)} reshape(f32[2,8,64,2048]{2,1,3,0:T(8,128)} %bitcast.142) | data formatting | bytes 16777216 | tf_op jit(solution)/shard_map/convert_element_type | solution.py:129
  201.0 5.8 multiply_multiply_fusion
  206.8 12.1 %subtract_convert_fusion = (bf16[2,512,16,64,1]{1,4,3,2,0:T(2,128)(2,1)}, bf16[2,512,16,64,1]{1,4,3,2,0:T(2,128)(2,1)}) fusion(f32[2,512,16,64,2]{1,4,3,2,0:T(2,128)S(1)} %multiply_multiply_fusion, f32[2,512,64]{1,2,0:T(8,128)S(1)} %get-tuple-element.46, f32[2,512,64]{1,2,0:T(8,128)S(1)} %get-tuple-element.45), kind=kLoop, calls=%fused_computation.26 | loop fusion | flops 8388608 | bytes 13107200 | tf_op jit(solution)/shard_map/convert.10
  225.5 4.8 subtract_convert_fusion.1
  233.0 10.1 %pad_maximum_fusion.1 = bf16[2,512,16,64,2]{1,4,3,2,0:T(2,128)(2,1)S(1)} fusion(bf16[2,512,16,64,1]{1,4,3,2,0:T(2,128)(2,1)} %get-tuple-element.29, bf16[2,512,16,64,1]{1,4,3,2,0:T(2,128)(2,1)} %get-tuple-element.28), kind=kLoop, calls=%fused_computation.24 | loop fusion | flops 8388608 | bytes 8388608 | tf_op jit(solution)/shard_map/stack | solution.py:30
  243.1 6.5 copy.117
  249.6 7.9 copy.118
  257.5 3.9 fusion.34
  264.3 3.5 fusion.6
  269.8 4.7 copy.129
  274.5 6.4 reshape.534
  287.4 7.2 multiply_reduce_fusion
  299.9 3.8 all-to-all-start.2
  305.5 3.1 fusion.13
  308.6 6.2 bitcast_add_fusion
  318.1 11.5 %copy.127 = f32[2,512,16,128]{3,2,1,0:T(8,128)} copy(f32[2,512,16,128]{3,1,2,0:T(8,128)} %bitcast_add_fusion) | data formatting | bytes 16777216 | tf_op jit(solution)/shard_map/add | solution.py:187
  329.5 9.3 %reshape_reshape.6 = f32[2,8,64,2048]{3,2,1,0:T(8,128)} reshape(f32[2,512,16,128]{3,2,1,0:T(8,128)} %copy.127) | data formatting | bytes 16777216 | tf_op jit(solution)/shard_map/reshape;reshape | solution.py:55
  338.9 7.8 copy.128
  347.6 5.3 all-to-all-start.1
  352.9 8.1 pad_maximum_fusion
  361.0 5.1 all-to-all-start
  366.7 194.6 %all-to-all-done = f32[8,132,2048]{2,1,0:T(8,128)} async-done(((f32[8,132,2048]{2,1,0:T(8,128)}), f32[8,132,2048]{2,1,0:T(8,128)}, u32[]{:S(2)}, u32[]{:S(2)}) %all-to-all-start) | async-done | bytes 8650784 | tf_op jit(solution)/shard_map/all_to_all | solution.py:215
  561.4 9.4 %reshape.575 = f32[8,132,16,128]{3,2,1,0:T(8,128)} reshape(f32[8,132,2048]{2,1,0:T(8,128)} %all-to-all-done) | data formatting | bytes 17301504 | tf_op jit(solution)/shard_map/reshape | solution.py:219
  570.8 5.4 fusion.2
  580.1 18.4 %all_to_all.34 = bf16[132,8,256]{2,0,1:T(8,128)(2,1)S(1)} all-to-all(bf16[132,8,256]{2,0,1:T(8,128)(2,1)S(1)} %copy.145), channel_id=1, replica_groups=mesh['dp'=4,'tensor'=8] {'tensor'}, dimensions={1} | all-to-all | bytes 1081344 | tf_op jit(solution)/shard_map/all_to_all | solution.py:228
  598.6 4.5 convolution_convert_fusion.1
  603.1 49.0 %fusion = bf16[136,2048]{1,0:T(8,128)(2,1)S(1)} fusion(bf16[1056,2048]{1,0:T(8,128)(2,1)} %convolution_convert_fusion.1), kind=kCustom, calls=%all-reduce-scatter | all-reduce-scatter fusion | flops 2228225 | bytes 4882944
  654.8 3.0 concatenate.44
  664.0 4.8 pad_maximum_fusion.2
  668.8 3.5 copy.148
  673.3 37.0 %all-gather.20.cloned.1.call-done = bf16[8,132,2048]{2,1,0:T(8,128)(2,1)} async-done(((bf16[1,132,2048]{2,1,0:T(8,128)(2,1)}), bf16[8,132,2048]{2,1,0:T(8,128)(2,1)}) %all-gather.20.cloned.1.call-update) | async-done | bytes 4325392 | tf_op jit(solution)/shard_map/all_gather | solution.py:64
  710.3 5.2 reshape.572
  715.4 13.3 %fusion.50 = f32[1056,2,1024]{2,0,1:T(8,128)S(1)} fusion(bf16[1056,2048,1]{1,0,2:T(8,128)(2,1)} %reshape.572, bf16[2,2048,1024]{2,1,0:T(8,128)(2,1)} %param.19), kind=kOutput, calls=%fused_computation.132 | convolution fusion | flops 8858370048 | bytes 21364736 | tf_op jit(solution)/shard_map/rd,kdc->rkc/dot_general | solution.py:62
  728.8 6.2 convolution_convert_fusion
  735.0 50.0 %fusion.1 = bf16[136,2048]{1,0:T(8,128)(2,1)} fusion(bf16[1056,2048]{1,0:T(8,128)(2,1)} %convolution_convert_fusion), kind=kCustom, calls=%all-reduce-scatter.1 | all-reduce-scatter fusion | flops 2228225 | bytes 4882944
  788.2 4.9 concatenate.45
  797.3 47.8 %all-gather.5 = bf16[32,4,2048]{2,1,0:T(4,128)(2,1)} all-gather(bf16[1,4,2048]{2,1,0:T(4,128)(2,1)S(1)} %slice_bitcast_fusion.3), channel_id=1, replica_groups=mesh['dp'=4,'tensor'=8] {'dp','tensor'}, dimensions={0}, use_global_device_ids=true | all-gather | bytes 540672 | tf_op jit(solution)/shard_map/all_gather | solution.py:236
  (195 shorter events, 70.7 us)
Async XLA Ops:
  7.2 60.5 %copy-start = (bf16[3,2048,256]{2,1,0:T(8,128)(2,1)S(1)}, bf16[3,2048,256]{2,1,0:T(8,128)(2,1)}, u32[]{:S(2)}) copy-start(bf16[3,2048,256]{2,1,0:T(8,128)(2,1)} %param.17) | copy-start | bytes 9437188
  7.2 55.3 %all-gather.18.cloned.1.call-start = ((), (), s32[]{:S(2)}) async-start(), calls=%async_computation.7 | async-start | bytes 5013504 | tf_op jit(solution)/shard_map/all_gather | solution.py:64
  9.3 113.2 %all-gather.12.cloned.1.call-start = ((), (), s32[]{:S(2)}) async-start(), calls=%async_computation.4 | async-start | bytes 4866048 | tf_op jit(solution)/shard_map/all_gather | solution.py:122
  73.4 2.1 copy-start.30
  73.4 2.4 copy-start.25
  73.4 2.4 copy-start.28
  73.5 2.6 copy-start.24
  74.7 97.2 %all-gather.14.cloned.1.call-start = ((), (), s32[]{:S(2)}) async-start(), calls=%async_computation.5 | async-start | bytes 4866048 | tf_op jit(solution)/shard_map/all_gather | solution.py:123
  75.4 228.3 %all-gather.16.cloned.1.call-start = ((), (), s32[]{:S(2)}) async-start(), calls=%async_computation.6 | async-start | bytes 4866048 | tf_op jit(solution)/shard_map/all_gather | solution.py:124
  77.2 123.9 %copy-start.12 = (f32[16,64,2]{2,1,0:T(8,128)}, f32[16,64,2]{2,1,0:T(8,128)S(1)}, u32[]{:S(2)}) copy-start(f32[16,64,2]{2,1,0:T(8,128)S(1)} %mul.338) | copy-start | bytes 24580
  127.7 6.8 copy-start.2
  230.3 12.8 %copy-start.4 = (bf16[132,16,64,1]{0,3,2,1:T(2,128)(2,1)}, bf16[132,16,64,1]{0,3,2,1:T(2,128)(2,1)S(1)}, u32[]{:S(2)}) copy-start(bf16[132,16,64,1]{0,3,2,1:T(2,128)(2,1)S(1)} %get-tuple-element.32) | copy-start | bytes 811012
  230.3 12.8 %copy-start.6 = (bf16[132,16,64,1]{0,3,2,1:T(2,128)(2,1)}, bf16[132,16,64,1]{0,3,2,1:T(2,128)(2,1)S(1)}, u32[]{:S(2)}) copy-start(bf16[132,16,64,1]{0,3,2,1:T(2,128)(2,1)S(1)} %get-tuple-element.33) | copy-start | bytes 811012
  231.5 11.6 %copy-start.9 = (bf16[128,16,64,2]{0,3,2,1:T(2,128)(2,1)}, bf16[128,16,64,2]{0,3,2,1:T(2,128)(2,1)S(1)}, u32[]{:S(2)}) copy-start(bf16[128,16,64,2]{0,3,2,1:T(2,128)(2,1)S(1)} %fusion.29) | copy-start | bytes 1572868
  257.5 3.9 copy-start.3
  257.5 3.9 copy-start.14
  261.4 1.6 copy-start.17
  264.3 3.5 copy-start.18
  274.5 7.6 copy-start.13
  274.5 9.0 %copy-start.21 = (f32[32,64]{0,1:T(8,128)S(1)}, f32[32,64]{0,1:T(8,128)}, u32[]{:S(2)}) copy-start(f32[32,64]{0,1:T(8,128)} %get-tuple-element.49) | copy-start | bytes 24580
  274.5 9.0 %copy-start.22 = (f32[32,64]{0,1:T(8,128)S(1)}, f32[32,64]{0,1:T(8,128)}, u32[]{:S(2)}) copy-start(f32[32,64]{0,1:T(8,128)} %get-tuple-element.50) | copy-start | bytes 24580
  287.4 8.7 %copy-start.5 = (bf16[132,16,64,1]{0,3,2,1:T(2,128)(2,1)S(1)}, bf16[132,16,64,1]{0,3,2,1:T(2,128)(2,1)}, u32[]{:S(2)}) copy-start(bf16[132,16,64,1]{0,3,2,1:T(2,128)(2,1)} %copy-done.4) | copy-start | bytes 811012
  287.4 8.7 %copy-start.7 = (bf16[132,16,64,1]{0,3,2,1:T(2,128)(2,1)S(1)}, bf16[132,16,64,1]{0,3,2,1:T(2,128)(2,1)}, u32[]{:S(2)}) copy-start(bf16[132,16,64,1]{0,3,2,1:T(2,128)(2,1)} %copy-done.6) | copy-start | bytes 811012
  299.9 47.8 %all-to-all-start.2 = ((f32[8,132,16]{1,2,0:T(8,128)}), f32[8,132,16]{1,2,0:T(8,128)S(1)}, u32[]{:S(2)}, u32[]{:S(2)}) async-start(f32[8,132,16]{1,2,0:T(8,128)} %pad_maximum_fusion.7), calls=%async_computation.2 | async-start | bytes 262144 | tf_op jit(solution)/shard_map/all_to_all | solution.py:214
  305.4 3.1 copy-start.16
  305.5 9.3 %slice-start = ((s8[6291456]{0:T(1024)(128)(4,1)}), s8[4194304]{0:T(1024)(128)(4,1)S(1)}, s32[]{:S(2)}) async-start(s8[6291456]{0:T(1024)(128)(4,1)} %bitcast.150), calls=%async_computation.9 | async-start | bytes 8388608
  308.6 6.3 slice-start.1
  314.8 2.8 copy-start.19
  347.6 13.4 %all-to-all-start.1 = ((f32[8,132,16]{1,2,0:T(8,128)}), f32[8,132,16]{1,2,0:T(8,128)S(1)}, u32[]{:S(2)}, u32[]{:S(2)}) async-start(f32[8,132,16]{1,2,0:T(8,128)} %pad_maximum_fusion.6), calls=%async_computation.1 | async-start | bytes 262144 | tf_op jit(solution)/shard_map/all_to_all | solution.py:213
  361.0 200.3 %all-to-all-start = ((f32[8,132,2048]{2,1,0:T(8,128)}), f32[8,132,2048]{2,1,0:T(8,128)}, u32[]{:S(2)}, u32[]{:S(2)}) async-start(f32[8,132,2048]{2,1,0:T(8,128)} %pad_maximum_fusion), calls=%async_computation | async-start | bytes 17825792 | tf_op jit(solution)/shard_map/all_to_all | solution.py:215
  366.1 344.1 %all-gather.20.cloned.1.call-start = ((), (), s32[]{:S(2)}) async-start(), calls=%async_computation.8 | async-start | bytes 5013504 | tf_op jit(solution)/shard_map/all_gather | solution.py:64
  603.1 50.4 %copy-start.27 = (u32[32]{0:T(128)S(1)}, u32[32]{0:T(128)}, u32[]{:S(2)}) copy-start(u32[32]{0:T(128)} %constant.85) | copy-start | bytes 388
  603.1 55.0 %copy-start.11 = (bf16[2,64,2048]{2,1,0:T(8,128)(2,1)S(1)}, bf16[2,64,2048]{2,1,0:T(8,128)(2,1)}, u32[]{:S(2)}) copy-start(bf16[2,64,2048]{2,1,0:T(8,128)(2,1)} %param.11) | copy-start | bytes 1572868
  603.1 55.0 %copy-start.20 = (bf16[4,2048]{1,0:T(4,128)(2,1)S(1)}, bf16[4,2048]{1,0:T(4,128)(2,1)}, u32[]{:S(2)}) copy-start(bf16[4,2048]{1,0:T(4,128)(2,1)} %param.12) | copy-start | bytes 49156
  603.1 56.2 %copy-start.26 = (s32[128]{0:T(128)S(1)}, s32[128]{0:T(128)}, u32[]{:S(2)}) copy-start(s32[128]{0:T(128)} %param.16) | copy-start | bytes 1540
  603.1 56.3 %copy-start.10 = (bf16[128,16,64,2]{0,3,2,1:T(2,128)(2,1)S(1)}, bf16[128,16,64,2]{0,3,2,1:T(2,128)(2,1)}, u32[]{:S(2)}) copy-start(bf16[128,16,64,2]{0,3,2,1:T(2,128)(2,1)} %copy-done.9) | copy-start | bytes 1572868
  652.2 2.6 copy-start.15
  652.2 2.6 collective-permute-start
  657.8 4.2 copy-start.8
  715.4 13.3 %copy-start.29 = (bf16[1024,2048]{1,0:T(8,128)(2,1)S(1)}, bf16[1024,2048]{1,0:T(8,128)(2,1)}, u32[]{:S(2)}) copy-start(bf16[1024,2048]{1,0:T(8,128)(2,1)} %param.20) | copy-start | bytes 12582916
  735.0 59.5 %copy-start.23 = (f32[1,2048]{1,0:T(1,128)S(1)}, f32[1,2048]{1,0:T(1,128)}, u32[]{:S(2)}) copy-start(f32[1,2048]{1,0:T(1,128)} %get-tuple-element.43) | copy-start | bytes 24580
  735.0 114.4 %copy-start.1 = (bf16[3,2048,256]{2,1,0:T(8,128)(2,1)S(1)}, bf16[3,2048,256]{2,1,0:T(8,128)(2,1)}, u32[]{:S(2)}) copy-start(bf16[3,2048,256]{2,1,0:T(8,128)(2,1)} %param.17) | copy-start | bytes 9437188
  785.9 2.3 collective-permute-start.1
Sparse Core Ops, SparseCore 0:
  10.2 52.2 all-gather.17
  74.8 47.6 all-gather.11
  124.7 47.1 all-gather.13
  173.3 47.1 all-gather.15
  659.4 50.8 all-gather.19
where the time goes:
time: 863 us; the launch traced here: 856 us
  waiting for transfers between devices  346 us (40%)
  local copies, waits for them, and re-layouts  166 us (19%)
  blocking collectives  165 us (19%)
  other arithmetic  99.2 us (11%)
  matrix products  47.6 us (6%)
  starting transfers between devices  16.9 us (2%)
  between operations  15.5 us (2%)
    all_to_all x1, waiting for transfers between devices, local(): lax.all_to_all(mixed, 'tensor', split_axis=0, concat_axis=0, tiled=True)  195 us
    unnamed x2, blocking collectives  99 us
    all_gather x2, waiting for transfers between devices, spread(): lax.all_gather(local_rows, 'tensor', axis=0, tiled=True)  90.1 us
    all_gather x1, blocking collectives, local(): lax.all_gather(output[prompt_own:], ('dp', 'tensor'), axis=0, tiled=True)  47.8 us
    unnamed x83, local copies, waits for them, and re-layouts  38.2 us
    all_gather x1, waiting for transfers between devices, local(): lax.all_gather(key_raw, 'tensor', axis=1, tiled=True)  36.5 us
    convert_element_type x2, local copies, waits for them, and re-layouts, local(): query_prompt.astype(jnp.float32)  27.6 us
    all_gather x1, waiting for transfers between devices, local(): lax.all_gather(query_raw, 'tensor', axis=1, tiled=True)  23.6 us
  transfers between devices with their start and end apart: 10, of which 6 were waited for; matrix products, arithmetic and copies ran while one was open for 27% of the time, Pallas kernels for 0%

commit v1 on v0

--- a/solution.py
+++ b/solution.py
@@ -1,6 +1,8 @@
 import jax
 import jax.numpy as jnp
 from jax import lax
+from jax.experimental import pallas as pl
+from jax.experimental.pallas import tpu as pltpu
 from jax.sharding import PartitionSpec as P
 
 HD = 128
@@ -245,6 +247,581 @@
     return (prompt_out, decode_out, new_prompt_kv, new_decode_kv)
 
 
+Z = 4
+BLOCK_PAD = 16
+
+
+def z_pairs(targets):
+    return [(z * 2 + c, t * 2 + c) for z in range(Z) for t in targets(z) for c in range(2)]
+
+
+CORE = [(i, i ^ 1) for i in range(2 * Z)]
+UP = [z_pairs(lambda z, k=k: [z + 1] if k <= z < Z - 1 else []) for k in range(Z - 1)]
+DOWN = [z_pairs(lambda z, k=k: [z - 1] if 0 < z <= Z - 1 - k else []) for k in range(Z - 1)]
+TURN = [z_pairs(lambda z, k=k: [(z + k) % Z]) for k in range(1, Z)]
+ENDS = z_pairs(lambda z: {0: [1], 3: [2]}.get(z, []))
+RISE = [z_pairs(lambda z: [z + 1] if z < 2 else []), z_pairs(lambda z: [z + 1] if z < 3 else [])]
+FALL = [z_pairs(lambda z: [z - 1] if z > 1 else []), z_pairs(lambda z: [z - 1] if z > 0 else [])]
+
+
+def send(values, pairs):
+    return lax.ppermute(values, "tensor", pairs)
+
+
+def line_gather(values, chip):
+    rising = falling = values
+    rises, falls = [], []
+    for step in range(Z - 1):
+        rising = send(rising, UP[step])
+        falling = send(falling, DOWN[step])
+        rises.append(rising)
+        falls.append(falling)
+    return [values] + [
+        jnp.where(chip >= k, rises[k - 1], falls[Z - 1 - k]) for k in range(1, Z)
+    ]
+
+
+def small_gather(values, chip, core):
+    pair = jnp.stack([values, send(values, CORE)])
+    pair = jnp.where(core == 0, pair, pair[::-1])
+    chips = jnp.stack([pair] + [send(pair, TURN[k]) for k in range(Z - 1)])
+    order = (chip - jnp.arange(Z, dtype=jnp.int32)) % Z
+    return jnp.take(chips, order, axis=0).reshape((2 * Z,) + values.shape)
+
+
+def small_sum(values):
+    total = values + send(values, CORE)
+    parts = [send(total, TURN[k]) for k in range(Z - 1)]
+    return total + parts[1] + (parts[0] + parts[2])
+
+
+def exchange(blocks, chip, core):
+    mine = lax.dynamic_index_in_dim(blocks, core, 1, keepdims=False)
+    other = lax.dynamic_index_in_dim(blocks, 1 - core, 1, keepdims=False)
+    both = jnp.stack([mine, send(other, CORE)], axis=1)
+    got = [lax.dynamic_index_in_dim(both, chip, 0, keepdims=False)]
+    for k in range(1, Z):
+        part = lax.dynamic_index_in_dim(both, (chip + k) % Z, 0, keepdims=False)
+        got.append(send(part, TURN[k - 1]))
+    return got
+
+
+def data_gather(values, data_pos):
+    first = jnp.stack([values, lax.ppermute(values, "dp", [(i, i ^ 1) for i in range(4)])])
+    second = lax.ppermute(first, "dp", [(i, i ^ 2) for i in range(4)])
+    both = jnp.concatenate([first, second])
+    return jnp.take(both, jnp.arange(4, dtype=jnp.int32) ^ data_pos, axis=0)
+
+
+def params(limit=56):
+    return pltpu.CompilerParams(vmem_limit_bytes=limit * 2**20)
+
+
+def project_kernel(where, xa, xb, w, pb_in, db_in, xs_in, prompt_out, decode_out, rows_out):
+    step = pl.program_id(0)
+
+    def work(x):
+        rows = x[...]
+        rows_out[0] = rows
+        for part in range(3):
+            made = jnp.dot(rows, w[part], preferred_element_type=jnp.float32)
+            made = made.astype(jnp.bfloat16)
+            cols = pl.ds(part * 256, 256)
+            prompt_out[0, 0, :, cols] = made[:64]
+            prompt_out[1, 0, :, cols] = made[64:128]
+            decode_out[0, :, cols] = made[128:]
+
+    @pl.when(step == 0)
+    def _():
+        work(xa)
+
+    @pl.when(step == 1)
+    def _():
+        work(xb)
+
+
+def project(where, xa, xb, w, buffers):
+    rows = xa.shape[0]
+    width = xa.shape[1]
+    grid_spec = pltpu.PrefetchScalarGridSpec(
+        num_scalar_prefetch=1,
+        grid=(2,),
+        in_specs=[
+            pl.BlockSpec((rows, width), lambda i, s: (0, 0)),
+            pl.BlockSpec((rows, width), lambda i, s: (0, 0)),
+            pl.BlockSpec(w.shape, lambda i, s: (0, 0, 0)),
+            pl.BlockSpec(memory_space=pl.ANY),
+            pl.BlockSpec(memory_space=pl.ANY),
+            pl.BlockSpec(memory_space=pl.ANY),
+        ],
+        out_specs=[
+            pl.BlockSpec((2, 1, 64, 768), lambda i, s: (0, s[i], 0, 0)),
+            pl.BlockSpec((1, rows - 128, 768), lambda i, s: (s[i], 0, 0)),
+            pl.BlockSpec((1, rows, width), lambda i, s: (s[i], 0, 0)),
+        ],
+    )
+    return pl.pallas_call(
+        project_kernel,
+        grid_spec=grid_spec,
+        out_shape=[jax.ShapeDtypeStruct(b.shape, b.dtype) for b in buffers],
+        input_output_aliases={4: 0, 5: 1, 6: 2},
+        compiler_params=params(),
+        cost_estimate=pl.CostEstimate(
+            flops=4 * rows * width * 768, bytes_accessed=9 * 2**20, transcendentals=0
+        ),
+        name="project",
+    )(where, xa, xb, w, *buffers)
+
+
+def swap_pairs(values):
+    lane = lax.broadcasted_iota(jnp.int32, values.shape, 1)
+    after = pltpu.roll(values, HD - 1, 1)
+    before = pltpu.roll(values, 1, 1)
+    return jnp.where(lane % 2 == 0, after, before)
+
+
+def attend_kernel(starts, q, k, v, ck, cv, scales, gain, cosine, sine, cached_at, out, key_out):
+    prompt = pl.program_id(0)
+    scale = scales[0]
+    cos_t, sin_t = cosine[0], sine[0]
+
+    def turn(raw, which):
+        val = raw[0].astype(jnp.float32) * scale[:, which : which + 1] * gain[which : which + 1, :]
+        return (val * cos_t + swap_pairs(val) * sin_t).astype(jnp.bfloat16)
+
+    queries = turn(q, 0)
+    keys = turn(k, 1)
+    key_out[0] = keys
+    dims = (((1,), (1,)), ((), ()))
+    factor = HD ** (-0.5)
+    rows = queries.shape[0]
+    old = lax.dot_general(queries, ck[0], dims, preferred_element_type=jnp.float32) * factor
+    new = lax.dot_general(queries, keys, dims, preferred_element_type=jnp.float32) * factor
+    live_old = cached_at[...] < starts[prompt]
+    live_new = lax.broadcasted_iota(jnp.int32, (rows, rows), 1) <= lax.broadcasted_iota(
+        jnp.int32, (rows, rows), 0
+    )
+    old = jnp.where(live_old, old, MASKED_SCORE)
+    new = jnp.where(live_new, new, MASKED_SCORE)
+    top = jnp.maximum(
+        jnp.max(old, axis=1, keepdims=True), jnp.max(new, axis=1, keepdims=True)
+    )
+    old = jnp.exp(old - top)
+    new = jnp.exp(new - top)
+    total = jnp.sum(old, axis=1, keepdims=True) + jnp.sum(new, axis=1, keepdims=True)
+    mixed = jnp.dot(old.astype(jnp.bfloat16), cv[0], preferred_element_type=jnp.float32)
+    mixed = mixed + jnp.dot(new.astype(jnp.bfloat16), v[0], preferred_element_type=jnp.float32)
+    out[0] = (mixed / total).astype(jnp.bfloat16)
+
+
+def attend(starts, qkv, ck, cv, scales, gain, cosine, sine, cached_at):
+    group = qkv.shape[1]
+    ctx = ck.shape[1]
+    head = lambda off: pl.BlockSpec((1, group, HD), lambda p, h, s: (p, 0, off + h))
+    grid_spec = pltpu.PrefetchScalarGridSpec(
+        num_scalar_prefetch=1,
+        grid=(2, 2),
+        in_specs=[
+            head(0),
+            head(2),
+            head(4),
+            pl.BlockSpec((1, ctx, HD), lambda p, h, s: (p, 0, h)),
+            pl.BlockSpec((1, ctx, HD), lambda p, h, s: (p, 0, h)),
+            pl.BlockSpec((1, group, 2), lambda p, h, s: (p, 0, 0)),
+            pl.BlockSpec((2, HD), lambda p, h, s: (0, h)),
+            pl.BlockSpec((1, group, HD), lambda p, h, s: (p, 0, 0)),
+            pl.BlockSpec((1, group, HD), lambda p, h, s: (p, 0, 0)),
+            pl.BlockSpec((1, ctx), lambda p, h, s: (0, 0)),
+        ],
+        out_specs=[head(0), head(0)],
+    )
+    made = jax.ShapeDtypeStruct((2, group, 2 * HD), jnp.bfloat16)
+    return pl.pallas_call(
+        attend_kernel,
+        grid_spec=grid_spec,
+        out_shape=[made, made],
+        compiler_params=params(),
+        cost_estimate=pl.CostEstimate(
+            flops=16 * group * (group + ctx) * HD,
+            bytes_accessed=6 * 2**20,
+            transcendentals=4 * group * (group + ctx),
+        ),
+        name="attend",
+    )(starts, qkv, qkv, qkv, ck, cv, scales, gain, cosine, sine, cached_at)
+
+
+def mix_kernel(where, *refs):
+    att = refs[:8]
+    wparts = refs[8:16]
+    dec, xs, dec_x, gain, out, lhs, w, sems = refs[16:]
+    step = pl.program_id(0)
+    data = where[8]
+
+    def copies():
+        made = []
+        for i in range(8):
+            cols = pl.ds(pl.multiple_of(where[i] * 256, 256), 256)
+            made.append(pltpu.make_async_copy(att[i], lhs.at[:, :, :, cols], sems.at[i]))
+        number = 8
+        for core in range(2):
+            for half in range(2):
+                for hop in range(2):
+                    part = wparts[core * 4 + half * 2 + hop]
+                    for lead in range(2):
+                        if half == 0:
+                            rel = lead + 2 * hop
+                        else:
+                            rel = 2 * lead + hop
+                        row = pl.multiple_of((data ^ rel) * 64, 64)
+                        for k in range(4):
+                            block = where[2 * k + core]
+                            made.append(
+                                pltpu.make_async_copy(
+                                    part.at[lead, k],
+                                    w.at[block, pl.ds(row, 64), pl.ds(half * 1024, 1024)],
+                                    sems.at[number],
+                                )
+                            )
+                            number += 1
+        return made
+
+    @pl.when(step == 0)
+    def _():
+        made = copies()
+        for copy in made:
+            copy.start()
+        for copy in made:
+            copy.wait()
+
+    pieces = []
+    for c in range(2):
+        pieces += [lhs[0, step * 2 + c], lhs[1, step * 2 + c], dec[c]]
+    rows = jnp.concatenate(pieces, axis=0)
+    total = jnp.zeros((rows.shape[0], w.shape[2]), jnp.float32)
+    for t in range(8):
+        total = total + jnp.dot(
+            rows[:, t * 256 : (t + 1) * 256], w[t], preferred_element_type=jnp.float32
+        )
+    inv = lax.rsqrt(jnp.mean(total * total, axis=1, keepdims=True) + EPSILON)
+    total = total * inv * gain[2:3, :]
+    per = 128 + BLOCK_PAD
+    for c in range(2):
+        base = c * per
+        out[c, :128] = (
+            xs[c, :128].astype(jnp.float32) + total[base : base + 128]
+        ).astype(jnp.bfloat16)
+        out[c, 128:] = (
+            dec_x[c].astype(jnp.float32) + total[base + 128 : base + per]
+        ).astype(jnp.bfloat16)
+
+
+def mix(where, att, wparts, dec, xs, dec_x, gains):
+    width = xs.shape[2]
+    any_spec = pl.BlockSpec(memory_space=pl.ANY)
+    grid_spec = pltpu.PrefetchScalarGridSpec(
+        num_scalar_prefetch=1,
+        grid=(Z,),
+        in_specs=[any_spec] * 16
+        + [
+            pl.BlockSpec((2, BLOCK_PAD, width), lambda i, s: (i, 0, 0)),
+            pl.BlockSpec((2, xs.shape[1], width), lambda i, s: (i, 0, 0)),
+            pl.BlockSpec((2, BLOCK_PAD, width), lambda i, s: (i, 0, 0)),
+            pl.BlockSpec(gains.shape, lambda i, s: (0, 0)),
+        ],
+        out_specs=pl.BlockSpec((2, 128 + BLOCK_PAD, width), lambda i, s: (i, 0, 0)),
+        scratch_shapes=[
+            pltpu.VMEM((2, 8, 64, width), jnp.bfloat16),
+            pltpu.VMEM((8, 256, width), jnp.bfloat16),
+            pltpu.SemaphoreType.DMA((8 + 64,)),
+        ],
+    )
+    return pl.pallas_call(
+        mix_kernel,
+        grid_spec=grid_spec,
+        out_shape=jax.ShapeDtypeStruct((8, 128 + BLOCK_PAD, width), jnp.bfloat16),
+        compiler_params=params(),
+        cost_estimate=pl.CostEstimate(
+            flops=2 * 8 * 144 * width * width, bytes_accessed=22 * 2**20, transcendentals=0
+        ),
+        name="mix",
+    )(where, *att, *wparts, dec, xs, dec_x, gains)
+
+
+def forward_kernel(where, hidden, wgu, wd, mine, other, acc):
+    step = pl.program_id(0)
+    per = hidden.shape[1]
+    rows = hidden[...].reshape(2 * per, hidden.shape[2])
+    gate = jnp.dot(rows, wgu[0], preferred_element_type=jnp.float32)
+    up = jnp.dot(rows, wgu[1], preferred_element_type=jnp.float32)
+    act = (gate / (1.0 + jnp.exp(-gate)) * up).astype(jnp.bfloat16)
+    part = jnp.dot(act, wd[...], preferred_element_type=jnp.float32).reshape(acc.shape)
+
+    @pl.when(step == 0)
+    def _():
+        acc[...] = part
+
+    @pl.when(step > 0)
+    def _():
+        acc[...] += part
+
+    @pl.when(step == pl.num_programs(0) - 1)
+    def _():
+        core = where[1]
+        mine[...] = acc[core, : mine.shape[0]].astype(jnp.bfloat16)
+        other[...] = acc[1 - core, : mine.shape[0]].astype(jnp.bfloat16)
+
+
+def forward(where, hidden, wgu, wd, rows):
+    per, width = hidden.shape[1:]
+    units = wd.shape[0]
+    tile = 256
+    grid_spec = pltpu.PrefetchScalarGridSpec(
+        num_scalar_prefetch=1,
+        grid=(units // tile,),
+        in_specs=[
+            pl.BlockSpec((2, per, width), lambda i, s: (s[0], 0, 0)),
+            pl.BlockSpec((2, width, tile), lambda i, s: (0, 0, i)),
+            pl.BlockSpec((tile, width), lambda i, s: (i, 0)),
+        ],
+        out_specs=[pl.BlockSpec((rows, width), lambda i, s: (0, 0))] * 2,
+        scratch_shapes=[pltpu.VMEM((2, per, width), jnp.float32)],
+    )
+    made = jax.ShapeDtypeStruct((rows, width), jnp.bfloat16)
+    return pl.pallas_call(
+        forward_kernel,
+        grid_spec=grid_spec,
+        out_shape=[made, made],
+        compiler_params=params(),
+        cost_estimate=pl.CostEstimate(
+            flops=12 * per * width * units, bytes_accessed=14 * 2**20, transcendentals=0
+        ),
+        name="forward",
+    )(where, hidden, wgu, wd)
+
+
+def tables(positions):
+    lanes = jnp.arange(HD, dtype=jnp.int32)
+    freq_index = (lanes // 2).astype(jnp.float32)
+    inv_freq = jnp.power(ROPE_BASE, -2.0 * freq_index / HD)
+    angles = positions.astype(jnp.float32)[..., None] * inv_freq
+    sign = jnp.where(lanes % 2 == 0, -1.0, 1.0)
+    return jnp.cos(angles), jnp.sin(angles) * sign
+
+
+def narrow_sum(*terms):
+    total = terms[0].astype(jnp.float32)
+    for term in terms[1:]:
+        total = total + term.astype(jnp.float32)
+    return total.astype(jnp.bfloat16)
+
+
+def after(values, *others):
+    return lax.optimization_barrier((values,) + others)[0]
+
+
+def local_heads(
+    prompt_states,
+    decode_states,
+    cache,
+    prompt_starts,
+    decode_lengths,
+    decode_slots,
+    w_qkv,
+    w_out,
+    w_gate_up,
+    w_down,
+    gains,
+):
+    place = lax.axis_index("tensor")
+    chip, core = place // 2, place % 2
+    data_pos = lax.axis_index("dp")
+    pre_dev, part_rows, width = prompt_states.shape
+    dec_part = decode_states.shape[0]
+    group = part_rows * 8
+    dec_dev = dec_part * 8
+    ctx_part = cache.shape[2]
+    heads = width // HD
+    own_rows = pre_dev * part_rows + dec_part
+    states = jnp.concatenate(
+        [prompt_states.reshape(pre_dev * part_rows, width), decode_states], axis=0
+    )
+    starts = lax.dynamic_slice_in_dim(prompt_starts, data_pos * pre_dev, pre_dev)
+    slot_ids = data_pos * dec_dev + jnp.arange(dec_dev, dtype=jnp.int32)
+    matches = decode_slots[None, :] == slot_ids[:, None]
+    slot_length = jnp.sum(jnp.where(matches, decode_lengths[None, :], 0), axis=1)
+    prompt_pos = starts[:, None] + jnp.arange(group, dtype=jnp.int32)[None, :]
+    cos_p, sin_p = tables(prompt_pos)
+    cos_d, sin_d = tables(slot_length)
+    my_gains = lax.dynamic_slice_in_dim(gains[:2], place * 256, 256, 1)
+
+    chips_at = (chip - jnp.arange(Z, dtype=jnp.int32)) % Z
+    blocks_at = jnp.stack([chips_at * 2 + core, chips_at * 2 + 1 - core], axis=1).astype(jnp.int32)
+    lines = line_gather(states, chip)
+    buffers = (
+        jnp.zeros((2, 8, 64, 768), jnp.bfloat16),
+        jnp.zeros((8, dec_part, 768), jnp.bfloat16),
+        jnp.zeros((8, own_rows, width), jnp.bfloat16),
+    )
+    for k in range(Z):
+        buffers = project(blocks_at[k], lines[k], send(lines[k], CORE), w_qkv, buffers)
+    prompt_raw, decode_raw, xs = buffers
+    prompt_raw = prompt_raw.reshape(pre_dev, group, 768)
+    decode_raw = decode_raw.reshape(dec_dev, 768)
+
+    prompt_cache = cache[:, :pre_dev].reshape(2, pre_dev, ctx_part, Z, 2, 256)
+    prompt_cache = jnp.transpose(prompt_cache, (3, 4, 0, 1, 2, 5))
+    prompt_cache = after(prompt_cache, lines[2])
+    got = exchange(prompt_cache, chip, core)
+    got = jnp.stack(got).reshape(8, 2, pre_dev, ctx_part, 256)
+    got = jnp.transpose(got, (1, 2, 0, 3, 4)).reshape(2, pre_dev, 8 * ctx_part, 256)
+    cached_at = (
+        blocks_at.reshape(8, 1) * ctx_part + jnp.arange(ctx_part, dtype=jnp.int32)[None, :]
+    ).reshape(1, 8 * ctx_part)
+
+    share = w_out.shape[0] // 4
+    w_share = lax.dynamic_slice_in_dim(w_out, data_pos * share, share)
+    w_share = after(w_share, lines[3])
+    w_line = jnp.stack(line_gather(w_share, chip))
+    half = width // 2
+    first, second = w_line[:, :, :half], w_line[:, :, half:]
+    along_x = lambda v: lax.ppermute(v, "dp", [(i, i ^ 1) for i in range(4)])
+    along_y = lambda v: lax.ppermute(v, "dp", [(i, i ^ 2) for i in range(4)])
+    first_pair = jnp.stack([first, along_x(first)])
+    second_pair = jnp.stack([second, along_y(second)])
+    w_own = [first_pair, along_y(first_pair), second_pair, along_x(second_pair)]
+    w_parts = w_own + [send(part, CORE) for part in w_own]
+
+    both = jnp.concatenate([prompt_raw.reshape(-1, 768), decode_raw])[:, :512].astype(jnp.float32)
+    squares = jnp.sum((both * both).reshape(-1, 2, 256), axis=-1)
+    squares = small_sum(jnp.swapaxes(squares, 0, 1))
+    scales = jnp.swapaxes(lax.rsqrt(squares / width + EPSILON), 0, 1)
+    prompt_rows = pre_dev * group
+    attended, key_new = attend(
+        starts,
+        prompt_raw,
+        got[0],
+        got[1],
+        scales[:prompt_rows].reshape(pre_dev, group, 2),
+        my_gains,
+        cos_p,
+        sin_p,
+        cached_at,
+    )
+
+    def turn(raw, scale, gain):
+        val = raw.astype(jnp.float32) * scale * gain
+        val = val.reshape(raw.shape[0], -1, HD)
+        pairs = val.reshape(val.shape[:-1] + (HD // 2, 2))
+        swapped = pairs[..., ::-1].reshape(val.shape)
+        return (val * cos_d[:, None] + swapped * sin_d[:, None]).astype(jnp.bfloat16)
+
+    dec_scales = scales[prompt_rows:]
+    query_mine = turn(decode_raw[:, :256], dec_scales[:, :1], my_gains[0])
+    key_mine = turn(decode_raw[:, 256:512], dec_scales[:, 1:], my_gains[1])
+    value_mine = decode_raw[:, 512:].reshape(dec_dev, 2, HD)
+    query_all = small_gather(query_mine.reshape(dec_dev, 256), chip, core)
+    query_all = jnp.swapaxes(query_all, 0, 1).reshape(dec_dev, heads, HD)
+    scale_factor = HD ** (-0.5)
+    decode_keys = cache[0, pre_dev:].reshape(dec_dev, ctx_part, heads, HD)
+    decode_values = cache[1, pre_dev:].reshape(dec_dev, ctx_part, heads, HD)
+    cache_pos = place * ctx_part + jnp.arange(ctx_part, dtype=jnp.int32)
+    live = (cache_pos[None, :] < slot_length[:, None])[:, None, :]
+    scores = jnp.einsum(
+        "she,sjhe->shj", query_all, decode_keys, preferred_element_type=jnp.float32
+    )
+    scores = jnp.where(live, scores * scale_factor, MASKED_SCORE)
+    tops = jnp.max(scores, axis=-1)
+    weights = jnp.where(live, jnp.exp(scores - tops[..., None]), 0.0)
+    sums = jnp.sum(weights, axis=-1)
+    mixed = jnp.einsum(
+        "shj,sjhe->she",
+        weights.astype(jnp.bfloat16),
+        decode_values,
+        preferred_element_type=jnp.float32,
+    )
+    parts = jnp.concatenate(
+        [
+            jnp.transpose(mixed.reshape(dec_dev, 8, 256), (1, 0, 2)),
+            jnp.transpose(tops.reshape(dec_dev, 8, 2), (1, 0, 2)),
+            jnp.transpose(sums.reshape(dec_dev, 8, 2), (1, 0, 2)),
+        ],
+        axis=-1,
+    )
+    arrived = exchange(parts.reshape(Z, 2, dec_dev, 260), chip, core)
+    arrived = jnp.stack(arrived).reshape(8, dec_dev, 260)
+    got_mixed = arrived[..., :256].reshape(8, dec_dev, 2, HD)
+    got_tops, got_sums = arrived[..., 256:258], arrived[..., 258:]
+    own_score = (
+        jnp.sum(query_mine.astype(jnp.float32) * key_mine.astype(jnp.float32), axis=-1)
+        * scale_factor
+    )
+    highest = jnp.maximum(jnp.max(got_tops, axis=0), own_score)
+    factors = jnp.exp(got_tops - highest[None])
+    own_weight = jnp.exp(own_score - highest)
+    total = jnp.sum(got_sums * factors, axis=0) + own_weight
+    summed = jnp.sum(got_mixed * factors[..., None], axis=0)
+    summed = summed + own_weight.astype(jnp.bfloat16).astype(jnp.float32)[
+        ..., None
+    ] * value_mine.astype(jnp.float32)
+    dec_attended = (summed / total[..., None]).reshape(dec_dev, 256).astype(jnp.bfloat16)
+    wanted = lax.dynamic_slice_in_dim(decode_slots, data_pos * dec_dev, dec_dev)
+    by_request = jnp.take(
+        data_gather(dec_attended, data_pos).reshape(4 * dec_dev, 256), wanted, axis=0
+    )
+    pad = lambda v: jnp.pad(
+        v.reshape(8, dec_part, width), ((0, 0), (0, BLOCK_PAD - dec_part), (0, 0))
+    )
+    dec_rows = small_gather(by_request, chip, core)
+    dec_rows = pad(jnp.swapaxes(dec_rows, 0, 1).reshape(dec_dev, width))
+    dec_x = data_gather(xs[:, own_rows - dec_part :].reshape(dec_dev, width), data_pos)
+    dec_x = pad(jnp.take(dec_x.reshape(4 * dec_dev, width), wanted, axis=0))
+
+    att_lines = line_gather(attended.reshape(pre_dev, 8, part_rows, 256), chip)
+    att = []
+    for line in att_lines:
+        att += [line, send(line, CORE)]
+    where = jnp.concatenate([blocks_at.reshape(8), data_pos[None].astype(jnp.int32)])
+    hidden = mix(where, att, w_parts, dec_rows, xs, dec_x, gains)
+
+    orders = jnp.array([[3, 2, 1, 0], [3, 2, 0, 1], [0, 1, 3, 2], [0, 1, 2, 3]], jnp.int32)
+    order = lax.dynamic_index_in_dim(orders, chip, 0, keepdims=False)
+    sums = []
+    for k in range(Z):
+        at = jnp.stack([order[k], core]).astype(jnp.int32)
+        mine, other = forward(at, hidden, w_gate_up, w_down, own_rows)
+        sums.append(narrow_sum(mine, send(other, CORE)))
+    came = send(sums[0], ENDS)
+    is_end = (chip == 0) | (chip == 3)
+    load = narrow_sum(jnp.where(is_end, sums[1], sums[0]), came)
+    up, down = send(load, RISE[0]), send(load, FALL[0])
+    up = send(narrow_sum(jnp.where(chip == 1, sums[1], sums[2]), up), RISE[1])
+    down = send(narrow_sum(jnp.where(chip == 2, sums[1], sums[2]), down), FALL[1])
+    ffn_sum = sums[3].astype(jnp.float32) + up.astype(jnp.float32) + down.astype(jnp.float32)
+    hidden_own = lax.dynamic_index_in_dim(hidden, place, 0, keepdims=False)[:own_rows]
+    output = (hidden_own.astype(jnp.float32) + rms_scale(ffn_sum, gains[3])).astype(jnp.bfloat16)
+    prompt_out = output[: own_rows - dec_part].reshape(pre_dev, part_rows, width)
+    decode_out = output[own_rows - dec_part :]
+
+    fresh = jnp.stack([key_new, prompt_raw[:, :, 512:]])
+    fresh = fresh.reshape(2, pre_dev, 8, part_rows, 256)
+    fresh = jnp.transpose(fresh, (2, 0, 1, 3, 4)).reshape(8, 2, pre_dev * part_rows, 256)
+    fresh_dec = jnp.stack([key_mine.reshape(dec_dev, 256), decode_raw[:, 512:]])
+    fresh_dec = jnp.transpose(fresh_dec.reshape(2, 8, dec_part, 256), (1, 0, 2, 3))
+    fresh = jnp.concatenate([fresh, fresh_dec], axis=2)
+    fresh = after(fresh, hidden)
+    came = exchange(fresh.reshape(Z, 2, 2, own_rows, 256), chip, core)
+    came = jnp.take(jnp.stack(came), chips_at, axis=0)
+    came = jnp.where(core == 0, came, came[:, ::-1]).reshape(8, 2, own_rows, 256)
+    came = jnp.transpose(came, (1, 2, 0, 3)).reshape(2, own_rows, width)
+    new_prompt_kv = came[:, : own_rows - dec_part].reshape(2, pre_dev, part_rows, width)
+    new_decode_kv = came[:, own_rows - dec_part :]
+    return (prompt_out, decode_out, new_prompt_kv, new_decode_kv)
+
+
+def fits_heads(mesh):
+    return mesh.shape["tensor"] == 2 * Z and mesh.shape["dp"] == 4
+
+
 def solution(mesh):
     in_specs = (
         P("dp", "tensor", None),
@@ -265,4 +842,5 @@
         P(None, "dp", "tensor", None),
         P(None, ("dp", "tensor"), None),
     )
-    return jax.shard_map(local, mesh=mesh, in_specs=in_specs, out_specs=out_specs, check_vma=False)
+    body = local_heads if fits_heads(mesh) else local
+    return jax.shard_map(body, mesh=mesh, in_specs=in_specs, out_specs=out_specs, check_vma=False)

time: 863 us -> 423 us (0.49)
  waiting for transfers between devices: 346 us -> 67.3 us
  blocking collectives: 165 us -> 0 us
  starting transfers between devices: 16.9 us -> 110 us
  Pallas kernels: 0 us -> 91 us
  local copies, waits for them, and re-layouts: 166 us -> 75.7 us
  other arithmetic: 99.2 us -> 59.1 us
  matrix products: 47.6 us -> 10.7 us
  between operations: 15.5 us -> 2.29 us
    all_to_all x3 -> x0, waiting for transfers between devices: 195 us -> none  [the longest x1 195 us: local(): lax.all_to_all(mixed, 'tensor', split_axis=0, concat_axis=0, tiled=True)]
    all_gather x5 -> x0, waiting for transfers between devices: 150 us -> none  [the longest x2 90.1 us: spread(): lax.all_gather(local_rows, 'tensor', axis=0, tiled=True)]
    ppermute x0 -> x71, starting transfers between devices: none -> 110 us  [the longest x63 99.3 us: send(): return lax.ppermute(values, 'tensor', pairs)]
    unnamed x2 -> x0, blocking collectives: 99 us -> none
    pallas_call x0 -> x10, Pallas kernels: none -> 91 us  [the longest x4 41 us: forward(): pl.pallas_call(forward_kernel, grid_spec=grid_spec, out_shape=[made, made...]
    ppermute x0 -> x71, waiting for transfers between devices: none -> 67.3 us  [the longest x63 62.6 us: send(): return lax.ppermute(values, 'tensor', pairs)]
    convert_element_type x7 -> x1, local copies, waits for them, and re-layouts: 48.8 us -> 0.09 us  [local_heads(): own_weight.astype(jnp.bfloat16).astype(jnp.float32)[..., None]]
    all_gather x1 -> x0, blocking collectives: 47.8 us -> none  [local(): lax.all_gather(output[prompt_own:], ('dp', 'tensor'), axis=0, tiled=True)]
  transfers between devices with their start and end apart: 10 -> 71, of which waited for: 6 -> 20; matrix products, arithmetic and copies ran while one was open for 27% -> 33% of each run, Pallas kernels for 0% -> 14%
where the time goes in v1:
time: 423 us; the launch traced here: 416 us
  starting transfers between devices  110 us (26%)
  Pallas kernels  91 us (22%)
  local copies, waits for them, and re-layouts  75.7 us (18%)
  waiting for transfers between devices  67.3 us (16%)
  other arithmetic  59.1 us (14%)
  matrix products  10.7 us (3%)
    ppermute x63, starting transfers between devices, send(): return lax.ppermute(values, 'tensor', pairs)  99.3 us
    ppermute x63, waiting for transfers between devices, send(): return lax.ppermute(values, 'tensor', pairs)  62.6 us
    pallas_call x4, Pallas kernels, forward(): pl.pallas_call(forward_kernel, grid_spec=grid_spec, out_shape=[made, made...  41 us
    pallas_call x1, Pallas kernels, mix(): pl.pallas_call(mix_kernel, grid_spec=grid_spec, out_shape=jax.ShapeDtypeS...  20.7 us
    pallas_call x4, Pallas kernels, project(): pl.pallas_call(project_kernel, grid_spec=grid_spec, out_shape=[jax.ShapeD...  20.4 us
    unnamed x106, local copies, waits for them, and re-layouts  16.1 us
    slice x1, local copies, waits for them, and re-layouts, local_heads(): decode_values = cache[1, pre_dev:].reshape(dec_dev, ctx_part, heads, HD)  10.7 us
    pallas_call x1, Pallas kernels, attend(): pl.pallas_call(attend_kernel, grid_spec=grid_spec, out_shape=[made, made]...  8.83 us
  transfers between devices with their start and end apart: 71, of which 20 were waited for; matrix products, arithmetic and copies ran while one was open for 33% of the time, Pallas kernels for 14%

profile of v1, /device:TPU:0, one launch (start us, length us, event | category | flops | bytes accessed | tf_op | source)
XLA Modules:
  0.0 415.6 jit_solution(2395005722721993547)
XLA Ops:
  4.4 5.9 %collective-permute-start = (bf16[132,2048]{1,0:T(8,128)(2,1)}, bf16[132,2048]{1,0:T(8,128)(2,1)}, u32[]{:S(2)}, u32[]{:S(2)}) collective-permute-start(bf16[132,2048]{1,0:T(8,128)(2,1)} %pad_maximum_fusion.8.xa), channel_id=1, source_target_pairs={{0,2},{1,3},{2,4},{3,5},{4,6},{5,7},{8,10},{9,11},{10,12},{11,13},... | collective-permute-start | bytes 1622024 | tf_op jit(solution)/shard_map/ppermute | solution.py:268
  11.3 10.7 %fusion.49 = (bf16[1,32,48,2048]{3,2,1,0:T(8,128)(2,1)}, bf16[1,32,48,2048]{3,2,1,0:T(8,128)(2,1)}) fusion(bf16[2,34,48,2048]{3,2,1,0:T(8,128)(2,1)} %param.16), kind=kLoop, calls=%fused_computation.216 | loop fusion | bytes 25165824 | tf_op jit(solution)/shard_map/slice | solution.py:726
  35.7 11.8 %collective-permute-done.5 = bf16[132,2048]{1,0:T(8,128)(2,1)} collective-permute-done((bf16[132,2048]{1,0:T(8,128)(2,1)S(1)}, bf16[132,2048]{1,0:T(8,128)(2,1)}, u32[]{:S(2)}, u32[]{:S(2)}) %collective-permute-start.5) | collective-permute-done | bytes 540704 | tf_op jit(solution)/shard_map/ppermute | solution.py:268
  53.1 3.0 fusion.6
  61.2 3.2 collective-permute-start.11
  64.4 2.8 collective-permute-start.12
  68.4 5.1 %collective-permute-done.7 = bf16[132,2048]{1,0:T(8,128)(2,1)S(1)} collective-permute-done((bf16[132,2048]{1,0:T(8,128)(2,1)}, bf16[132,2048]{1,0:T(8,128)(2,1)S(1)}, u32[]{:S(2)}, u32[]{:S(2)}) %collective-permute-start.7) | collective-permute-done | bytes 540704 | tf_op jit(solution)/shard_map/ppermute | solution.py:268
  80.9 7.9 %copy.373 = bf16[192,8,16,128]{3,2,1,0:T(8,128)(2,1)} copy(bf16[192,8,16,128]{3,1,2,0:T(8,128)(2,1)} %bitcast.222) | data formatting | bytes 12582912
  88.8 5.0 %copy.374 = bf16[192,8,16,128]{3,2,1,0:T(8,128)(2,1)} copy(bf16[192,8,16,128]{3,1,2,0:T(8,128)(2,1)S(1)} %bitcast.221) | data formatting | bytes 12582912
  93.9 2.6 broadcast_in_dim.151.clone.xs_in
  98.4 5.1 %project.4 = (bf16[2,8,64,768]{3,2,1,0:T(8,128)(2,1)}, bf16[8,4,768]{2,1,0:T(4,128)(2,1)}, bf16[8,132,2048]{2,1,0:T(8,128)(2,1)}) custom-call(s32[2]{0:T(128)} %get-tuple-element.55.where, bf16[132,2048]{1,0:T(8,128)(2,1)} %pad_maximum_fusion.8.xa, ...), custom_call_target="tpu_custom_call", output_to_operand_aliasing={{0}: (4, {}), {1}: (5, {}), {2}: (6, {})} | custom-call | flops 830472192 | bytes 9437184 | tf_op jit(solution)/shard_map/project/pallas_call | solution.py:363
  103.5 7.5 %collective-permute-start.28 = (bf16[64,2048]{1,0:T(8,128)(2,1)S(1)}, bf16[64,2048]{1,0:T(8,128)(2,1)}, u32[]{:S(2)}, u32[]{:S(2)}) collective-permute-start(bf16[64,2048]{1,0:T(8,128)(2,1)S(1)} %constant_dynamic-slice_fusion.5), channel_id=1, source_target_pairs={{0,2},{1,3},{2,4},{3,5},{4,6},{5,7},{8,10},{9,11},{10,12},{11,13},... | collective-permute-start | bytes 786440 | tf_op jit(solution)/shard_map/ppermute | solution.py:268
  112.4 2.1 pad_maximum_fusion.7
  118.0 5.1 %project.5 = (bf16[2,8,64,768]{3,2,1,0:T(8,128)(2,1)}, bf16[8,4,768]{2,1,0:T(4,128)(2,1)}, bf16[8,132,2048]{2,1,0:T(8,128)(2,1)}) custom-call(s32[2]{0:T(128)} %get-tuple-element.56.where, bf16[132,2048]{1,0:T(8,128)(2,1)} %copy-done.8, bf16[132,2048]{1,0:T(8,128)(2,1)} %collective-permute-done.8.xb, ...), custom_call_target="tpu_custom_call", output_to_operand_aliasing={{0}: (4, {}), {1}: (5, {}), {2}: (6, {})} | custom-call | flops 830472192 | bytes 9437184 | tf_op jit(solution)/shard_map/project/pallas_call | solution.py:363
  123.0 5.1 %project.6 = (bf16[2,8,64,768]{3,2,1,0:T(8,128)(2,1)}, bf16[8,4,768]{2,1,0:T(4,128)(2,1)}, bf16[8,132,2048]{2,1,0:T(8,128)(2,1)}) custom-call(s32[2]{0:T(128)} %get-tuple-element.57.where, bf16[132,2048]{1,0:T(8,128)(2,1)} %copy-done.6, bf16[132,2048]{1,0:T(8,128)(2,1)} %collective-permute-done.6.xb, ...), custom_call_target="tpu_custom_call", output_to_operand_aliasing={{0}: (4, {}), {1}: (5, {}), {2}: (6, {})} | custom-call | flops 830472192 | bytes 9437184 | tf_op jit(solution)/shard_map/project/pallas_call | solution.py:363
  128.2 5.1 %project.7 = (bf16[2,8,64,768]{3,2,1,0:T(8,128)(2,1)}, bf16[8,4,768]{2,1,0:T(4,128)(2,1)}, bf16[8,132,2048]{2,1,0:T(8,128)(2,1)}) custom-call(s32[2]{0:T(128)} %get-tuple-element.58.where, bf16[132,2048]{1,0:T(8,128)(2,1)} %copy-done.7, bf16[132,2048]{1,0:T(8,128)(2,1)} %collective-permute-done.4.xb, ...), custom_call_target="tpu_custom_call", output_to_operand_aliasing={{0}: (4, {}), {1}: (5, {}), {2}: (6, {})} | custom-call | flops 830472192 | bytes 9437184 | tf_op jit(solution)/shard_map/project/pallas_call | solution.py:363
  134.1 2.9 convert_multiply_fusion
  137.0 2.8 reshape.569
  139.8 2.7 reduce_sum.63
  148.5 14.7 %collective-permute-start.15 = (f32[2,1056]{1,0:T(2,128)S(1)}, f32[2,1056]{1,0:T(2,128)S(1)}, u32[]{:S(2)}, u32[]{:S(2)}) collective-permute-start(f32[2,1056]{1,0:T(2,128)S(1)} %bitcast_add_fusion), channel_id=1, source_target_pairs={{0,4},{1,5},{2,6},{3,7},{4,0},{5,1},{6,2},{7,3},{8,12},{9,13},{10,... | collective-permute-start | bytes 25352 | tf_op jit(solution)/shard_map/ppermute | solution.py:268
  163.1 3.8 collective-permute-start.17
  177.4 8.8 %attend.1 = (bf16[2,512,256]{2,1,0:T(8,128)(2,1)}, bf16[2,512,256]{2,1,0:T(8,128)(2,1)}) custom-call(s32[2]{0:T(128)} %copy-done.42, bf16[2,512,768]{2,1,0:T(8,128)(2,1)} %bitcast.216, bf16[2,512,768]{2,1,0:T(8,128)(2,1)} %bitcast.217, bf16[2,512,768]{2,1,0:T(8,128)(2,1)} %bitcast.218, bf16[2,384,256]{2,1,0:T(8,128)(2,1)} %bitcast.235, ...), custom_call_target="tpu_custom_call" | custom-call | flops 939524096 | bytes 6291456 | tf_op jit(solution)/shard_map/attend/pallas_call | solution.py:439
  186.3 3.4 collective-permute-start.43
  189.7 2.4 collective-permute-start.45
  194.8 3.2 collective-permute-start.19
  199.0 6.1 %fusion.2 = f32[32,16,1,48]{3,2,1,0:T(1,128)S(1)} fusion(bf16[32,16,128,1]{2,3,1,0:T(2,128)(2,1)S(1)} %reshape.664, bf16[32,48,16,128]{3,2,1,0:T(8,128)(2,1)} %bitcast.225), kind=kOutput, calls=%fused_computation.9 | convolution fusion | flops 6291456 | bytes 6520832 | tf_op jit(solution)/shard_map/she,sjhe->shj/dot_general | solution.py:729
  205.6 4.5 %fusion = f32[32,16,1,128]{3,2,1,0:T(1,128)S(1)} fusion(bf16[32,48,16,128]{3,2,1,0:T(8,128)(2,1)} %bitcast.224, bf16[32,16,48,1]{2,1,0,3:T(8,128)(2,1)S(1)} %get-tuple-element.90), kind=kOutput, calls=%fused_computation.7 | convolution fusion | flops 6291456 | bytes 6602752 | tf_op jit(solution)/shard_map/shj,sjhe->she/dot_general | solution.py:736
  215.5 3.5 collective-permute-start.49
  237.5 2.5 collective-permute-start.53
  244.4 4.1 collective-permute-done.54
  252.7 3.0 collective-permute-done.36
  266.9 4.8 %collective-permute-done.21 = bf16[2,8,64,256]{3,2,1,0:T(8,128)(2,1)} collective-permute-done((bf16[2,8,64,256]{3,2,1,0:T(8,128)(2,1)}, bf16[2,8,64,256]{3,2,1,0:T(8,128)(2,1)}, u32[]{:S(2)}, u32[]{:S(2)}) %collective-permute-start.21) | collective-permute-done | bytes 524320 | tf_op jit(solution)/shard_map/ppermute | solution.py:268
  276.3 8.1 %collective-permute-done.22 = bf16[2,8,64,256]{3,2,1,0:T(8,128)(2,1)S(1)} collective-permute-done((bf16[2,8,64,256]{3,2,1,0:T(8,128)(2,1)}, bf16[2,8,64,256]{3,2,1,0:T(8,128)(2,1)S(1)}, u32[]{:S(2)}, u32[]{:S(2)}) %collective-permute-start.22) | collective-permute-done | bytes 524320 | tf_op jit(solution)/shard_map/ppermute | solution.py:268
  288.6 3.3 collective-permute-done.27.refs_7_
  292.7 20.7 %mix.1.hidden = bf16[8,144,2048]{2,1,0:T(8,128)(2,1)} custom-call(s32[9]{0:T(128)} %pad_add_fusion.1.where, bf16[2,8,64,256]{3,2,1,0:T(8,128)(2,1)} %bitcast.21.refs_0_, bf16[2,8,64,256]{3,2,1,0:T(8,128)(2,1)} %collective-permute-done.18.refs_1_, bf16[2,8,64,256]{3,2,1,0:T(8,128)(2,1)} %broadcast_select_fusion.7.refs_2_, bf16[2,8,64,256]{3,2,1,0:T(8,128)(2,1)} %copy-done.47, ...), custom_call_target="tpu_custom_call" | custom-call | flops 9663676416 | bytes 23068672 | tf_op jit(solution)/shard_map/mix/pallas_call | solution.py:538
  313.5 10.3 %forward.7 = (bf16[132,2048]{1,0:T(8,128)(2,1)}, bf16[132,2048]{1,0:T(8,128)(2,1)}) custom-call(s32[2]{0:T(128)} %get-tuple-element.117.where, bf16[8,144,2048]{2,1,0:T(8,128)(2,1)} %mix.1.hidden, bf16[2,2048,1024]{2,1,0:T(8,128)(2,1)} %wgu.7, bf16[1024,2048]{1,0:T(8,128)(2,1)} %wd.7), custom_call_target="tpu_custom_call" | custom-call | flops 3623878656 | bytes 14680064 | tf_op jit(solution)/shard_map/forward/pallas_call | solution.py:590
  326.1 10.3 %forward.5 = (bf16[132,2048]{1,0:T(8,128)(2,1)}, bf16[132,2048]{1,0:T(8,128)(2,1)}) custom-call(s32[2]{0:T(128)} %get-tuple-element.115.where, bf16[8,144,2048]{2,1,0:T(8,128)(2,1)} %mix.1.hidden, bf16[2,2048,1024]{2,1,0:T(8,128)(2,1)} %wgu.7, bf16[1024,2048]{1,0:T(8,128)(2,1)} %wd.7), custom_call_target="tpu_custom_call" | custom-call | flops 3623878656 | bytes 14680064 | tf_op jit(solution)/shard_map/forward/pallas_call | solution.py:590
  338.4 10.1 %forward.6 = (bf16[132,2048]{1,0:T(8,128)(2,1)}, bf16[132,2048]{1,0:T(8,128)(2,1)}) custom-call(s32[2]{0:T(128)} %get-tuple-element.116.where, bf16[8,144,2048]{2,1,0:T(8,128)(2,1)} %mix.1.hidden, bf16[2,2048,1024]{2,1,0:T(8,128)(2,1)} %wgu.7, bf16[1024,2048]{1,0:T(8,128)(2,1)} %wd.7), custom_call_target="tpu_custom_call" | custom-call | flops 3623878656 | bytes 14680064 | tf_op jit(solution)/shard_map/forward/pallas_call | solution.py:590
  350.4 2.0 collective-permute-start.70
  354.3 6.5 %collective-permute-start.63 = (bf16[132,2048]{1,0:T(8,128)(2,1)}, bf16[132,2048]{1,0:T(8,128)(2,1)}, u32[]{:S(2)}, u32[]{:S(2)}) collective-permute-start(bf16[132,2048]{1,0:T(8,128)(2,1)} %add_convert_fusion.2), channel_id=1, source_target_pairs={{0,2},{1,3},{2,4},{3,5},{8,10},{9,11},{10,12},{11,13},{16,18},{17,... | collective-permute-start | bytes 1622024 | tf_op jit(solution)/shard_map/ppermute | solution.py:268
  360.7 5.9 %collective-permute-done.70 = bf16[2,2,132,256]{3,1,2,0:T(2,128)(2,1)S(1)} collective-permute-done((bf16[2,2,132,256]{3,1,2,0:T(2,128)(2,1)S(1)}, bf16[2,2,132,256]{3,1,2,0:T(2,128)(2,1)S(1)}, u32[]{:S(2)}, u32[]{:S(2)}) %collective-permute-start.70) | collective-permute-done | bytes 270368 | tf_op jit(solution)/shard_map/ppermute | solution.py:268
  368.1 10.2 %forward.4 = (bf16[132,2048]{1,0:T(8,128)(2,1)}, bf16[132,2048]{1,0:T(8,128)(2,1)}) custom-call(s32[2]{0:T(128)} %get-tuple-element.114.where, bf16[8,144,2048]{2,1,0:T(8,128)(2,1)} %mix.1.hidden, bf16[2,2048,1024]{2,1,0:T(8,128)(2,1)} %wgu.7, bf16[1024,2048]{1,0:T(8,128)(2,1)} %wd.7), custom_call_target="tpu_custom_call" | custom-call | flops 3623878656 | bytes 14680064 | tf_op jit(solution)/shard_map/forward/pallas_call | solution.py:590
  380.4 2.8 gather_fusion.4
  383.3 3.4 add_convert_fusion.1
  386.6 6.8 %collective-permute-start.64 = (bf16[132,2048]{1,0:T(8,128)(2,1)}, bf16[132,2048]{1,0:T(8,128)(2,1)S(1)}, u32[]{:S(2)}, u32[]{:S(2)}) collective-permute-start(bf16[132,2048]{1,0:T(8,128)(2,1)} %get-tuple-element.65), channel_id=1, source_target_pairs={{0,2},{1,3},{2,4},{3,5},{4,6},{5,7},{8,10},{9,11},{10,12},{11,13},... | collective-permute-start | bytes 1622024 | tf_op jit(solution)/shard_map/ppermute | solution.py:268
  399.3 5.9 %collective-permute-done.64 = bf16[132,2048]{1,0:T(8,128)(2,1)S(1)} collective-permute-done((bf16[132,2048]{1,0:T(8,128)(2,1)}, bf16[132,2048]{1,0:T(8,128)(2,1)S(1)}, u32[]{:S(2)}, u32[]{:S(2)}) %collective-permute-start.64) | collective-permute-done | bytes 540704 | tf_op jit(solution)/shard_map/ppermute | solution.py:268
  405.2 4.9 %collective-permute-done.66 = bf16[132,2048]{1,0:T(8,128)(2,1)} collective-permute-done((bf16[132,2048]{1,0:T(8,128)(2,1)}, bf16[132,2048]{1,0:T(8,128)(2,1)}, u32[]{:S(2)}, u32[]{:S(2)}) %collective-permute-start.66) | collective-permute-done | bytes 540704 | tf_op jit(solution)/shard_map/ppermute | solution.py:268
  411.7 2.2 fusion.4
  (400 shorter events, 138.5 us)
Async XLA Ops:
  2.7 73.1 %collective-permute-start.9 = (bf16[132,2048]{1,0:T(8,128)(2,1)}, bf16[132,2048]{1,0:T(8,128)(2,1)}, u32[]{:S(2)}, u32[]{:S(2)}) collective-permute-start(bf16[132,2048]{1,0:T(8,128)(2,1)} %pad_maximum_fusion.8.xa), channel_id=1, source_target_pairs={{0,1},{1,0},{2,3},{3,2},{4,5},{5,4},{6,7},{7,6},{8,9},{9,8},{10,11... | collective-permute-start | bytes 1622024 | tf_op jit(solution)/shard_map/ppermute | solution.py:268
  3.1 27.7 %collective-permute-start.3 = (bf16[132,2048]{1,0:T(8,128)(2,1)}, bf16[132,2048]{1,0:T(8,128)(2,1)S(1)}, u32[]{:S(2)}, u32[]{:S(2)}) collective-permute-start(bf16[132,2048]{1,0:T(8,128)(2,1)} %pad_maximum_fusion.8.xa), channel_id=1, source_target_pairs={{2,0},{3,1},{4,2},{5,3},{6,4},{7,5},{10,8},{11,9},{12,10},{13,11},... | collective-permute-start | bytes 1622024 | tf_op jit(solution)/shard_map/ppermute | solution.py:268
  4.4 27.7 %collective-permute-start = (bf16[132,2048]{1,0:T(8,128)(2,1)}, bf16[132,2048]{1,0:T(8,128)(2,1)}, u32[]{:S(2)}, u32[]{:S(2)}) collective-permute-start(bf16[132,2048]{1,0:T(8,128)(2,1)} %pad_maximum_fusion.8.xa), channel_id=1, source_target_pairs={{0,2},{1,3},{2,4},{3,5},{4,6},{5,7},{8,10},{9,11},{10,12},{11,13},... | collective-permute-start | bytes 1622024 | tf_op jit(solution)/shard_map/ppermute | solution.py:268
  30.8 16.7 %collective-permute-start.5 = (bf16[132,2048]{1,0:T(8,128)(2,1)S(1)}, bf16[132,2048]{1,0:T(8,128)(2,1)}, u32[]{:S(2)}, u32[]{:S(2)}) collective-permute-start(bf16[132,2048]{1,0:T(8,128)(2,1)S(1)} %collective-permute-done.3), channel_id=1, source_target_pairs={{2,0},{3,1},{4,2},{5,3},{10,8},{11,9},{12,10},{13,11},{18,16},{19,... | collective-permute-start | bytes 1622024 | tf_op jit(solution)/shard_map/ppermute | solution.py:268
  32.1 15.5 %collective-permute-start.1 = (bf16[132,2048]{1,0:T(8,128)(2,1)}, bf16[132,2048]{1,0:T(8,128)(2,1)}, u32[]{:S(2)}, u32[]{:S(2)}) collective-permute-start(bf16[132,2048]{1,0:T(8,128)(2,1)} %collective-permute-done), channel_id=1, source_target_pairs={{2,4},{3,5},{4,6},{5,7},{10,12},{11,13},{12,14},{13,15},{18,20},{1... | collective-permute-start | bytes 1622024 | tf_op jit(solution)/shard_map/ppermute | solution.py:268
  51.2 22.2 %collective-permute-start.7 = (bf16[132,2048]{1,0:T(8,128)(2,1)}, bf16[132,2048]{1,0:T(8,128)(2,1)S(1)}, u32[]{:S(2)}, u32[]{:S(2)}) collective-permute-start(bf16[132,2048]{1,0:T(8,128)(2,1)} %collective-permute-done.5), channel_id=1, source_target_pairs={{2,0},{3,1},{10,8},{11,9},{18,16},{19,17},{26,24},{27,25}} | collective-permute-start | bytes 1622024 | tf_op jit(solution)/shard_map/ppermute | solution.py:268
  56.1 19.4 %collective-permute-start.2 = (bf16[132,2048]{1,0:T(8,128)(2,1)}, bf16[132,2048]{1,0:T(8,128)(2,1)S(1)}, u32[]{:S(2)}, u32[]{:S(2)}) collective-permute-start(bf16[132,2048]{1,0:T(8,128)(2,1)} %collective-permute-done.1), channel_id=1, source_target_pairs={{4,6},{5,7},{12,14},{13,15},{20,22},{21,23},{28,30},{29,31}} | collective-permute-start | bytes 1622024 | tf_op jit(solution)/shard_map/ppermute | solution.py:268
  61.2 15.1 %collective-permute-start.11 = (bf16[2,2,2,48,256]{4,0,3,2,1:T(2,128)(2,1)S(1)}, bf16[2,2,2,48,256]{4,0,3,2,1:T(2,128)(2,1)S(1)}, u32[]{:S(2)}, u32[]{:S(2)}) collective-permute-start(bf16[2,2,2,48,256]{4,0,3,2,1:T(2,128)(2,1)S(1)} %get-tuple-element.68), channel_id=1, source_target_pairs={{0,2},{1,3},{2,4},{3,5},{4,6},{5,7},{6,0},{7,1},{8,10},{9,11},{10,... | collective-permute-start | bytes 589832 | tf_op jit(solution)/shard_map/ppermute | solution.py:268
  64.4 39.1 %collective-permute-start.12 = (bf16[2,2,2,48,256]{4,0,3,2,1:T(2,128)(2,1)}, bf16[2,2,2,48,256]{4,0,3,2,1:T(2,128)(2,1)}, u32[]{:S(2)}, u32[]{:S(2)}) collective-permute-start(bf16[2,2,2,48,256]{4,0,3,2,1:T(2,128)(2,1)} %get-tuple-element.69), channel_id=1, source_target_pairs={{0,4},{1,5},{2,6},{3,7},{4,0},{5,1},{6,2},{7,3},{8,12},{9,13},{10,... | collective-permute-start | bytes 589832 | tf_op jit(solution)/shard_map/ppermute | solution.py:268
  74.2 36.8 %collective-permute-start.13 = (bf16[2,2,2,48,256]{4,0,3,2,1:T(2,128)(2,1)}, bf16[2,2,2,48,256]{4,0,3,2,1:T(2,128)(2,1)S(1)}, u32[]{:S(2)}, u32[]{:S(2)}) collective-permute-start(bf16[2,2,2,48,256]{4,0,3,2,1:T(2,128)(2,1)} %fusion.16), channel_id=1, source_target_pairs={{0,6},{1,7},{2,0},{3,1},{4,2},{5,3},{6,4},{7,5},{8,14},{9,15},{10,... | collective-permute-start | bytes 589832 | tf_op jit(solution)/shard_map/ppermute | solution.py:268
  75.6 42.4 %collective-permute-start.8 = (bf16[132,2048]{1,0:T(8,128)(2,1)S(1)}, bf16[132,2048]{1,0:T(8,128)(2,1)}, u32[]{:S(2)}, u32[]{:S(2)}) collective-permute-start(bf16[132,2048]{1,0:T(8,128)(2,1)S(1)} %broadcast_select_fusion.2.xa), channel_id=1, source_target_pairs={{0,1},{1,0},{2,3},{3,2},{4,5},{5,4},{6,7},{7,6},{8,9},{9,8},{10,11... | collective-permute-start | bytes 1622024 | tf_op jit(solution)/shard_map/ppermute | solution.py:268
  75.8 47.3 %collective-permute-start.6 = (bf16[132,2048]{1,0:T(8,128)(2,1)S(1)}, bf16[132,2048]{1,0:T(8,128)(2,1)}, u32[]{:S(2)}, u32[]{:S(2)}) collective-permute-start(bf16[132,2048]{1,0:T(8,128)(2,1)S(1)} %broadcast_select_fusion.3.xa), channel_id=1, source_target_pairs={{0,1},{1,0},{2,3},{3,2},{4,5},{5,4},{6,7},{7,6},{8,9},{9,8},{10,11... | collective-permute-start | bytes 1622024 | tf_op jit(solution)/shard_map/ppermute | solution.py:268
  76.3 51.8 %collective-permute-start.4 = (bf16[132,2048]{1,0:T(8,128)(2,1)S(1)}, bf16[132,2048]{1,0:T(8,128)(2,1)}, u32[]{:S(2)}, u32[]{:S(2)}) collective-permute-start(bf16[132,2048]{1,0:T(8,128)(2,1)S(1)} %broadcast_select_fusion.4.xa), channel_id=1, source_target_pairs={{0,1},{1,0},{2,3},{3,2},{4,5},{5,4},{6,7},{7,6},{8,9},{9,8},{10,11... | collective-permute-start | bytes 1622024 | tf_op jit(solution)/shard_map/ppermute | solution.py:268
  103.5 13.1 %collective-permute-start.28 = (bf16[64,2048]{1,0:T(8,128)(2,1)S(1)}, bf16[64,2048]{1,0:T(8,128)(2,1)}, u32[]{:S(2)}, u32[]{:S(2)}) collective-permute-start(bf16[64,2048]{1,0:T(8,128)(2,1)S(1)} %constant_dynamic-slice_fusion.5), channel_id=1, source_target_pairs={{0,2},{1,3},{2,4},{3,5},{4,6},{5,7},{8,10},{9,11},{10,12},{11,13},... | collective-permute-start | bytes 786440 | tf_op jit(solution)/shard_map/ppermute | solution.py:268
  111.1 34.3 %collective-permute-start.29 = (bf16[64,2048]{1,0:T(8,128)(2,1)S(1)}, bf16[64,2048]{1,0:T(8,128)(2,1)}, u32[]{:S(2)}, u32[]{:S(2)}) collective-permute-start(bf16[64,2048]{1,0:T(8,128)(2,1)S(1)} %constant_dynamic-slice_fusion.5), channel_id=1, source_target_pairs={{2,0},{3,1},{4,2},{5,3},{6,4},{7,5},{10,8},{11,9},{12,10},{13,11},... | collective-permute-start | bytes 786440 | tf_op jit(solution)/shard_map/ppermute | solution.py:268
  116.6 30.5 %collective-permute-start.32 = (bf16[64,2048]{1,0:T(8,128)(2,1)}, bf16[64,2048]{1,0:T(8,128)(2,1)}, u32[]{:S(2)}, u32[]{:S(2)}) collective-permute-start(bf16[64,2048]{1,0:T(8,128)(2,1)} %collective-permute-done.28), channel_id=1, source_target_pairs={{2,4},{3,5},{4,6},{5,7},{10,12},{11,13},{12,14},{13,15},{18,20},{1... | collective-permute-start | bytes 786440 | tf_op jit(solution)/shard_map/ppermute | solution.py:268
  145.4 21.6 %collective-permute-start.30 = (bf16[64,2048]{1,0:T(8,128)(2,1)}, bf16[64,2048]{1,0:T(8,128)(2,1)}, u32[]{:S(2)}, u32[]{:S(2)}) collective-permute-start(bf16[64,2048]{1,0:T(8,128)(2,1)} %collective-permute-done.29), channel_id=1, source_target_pairs={{2,0},{3,1},{4,2},{5,3},{10,8},{11,9},{12,10},{13,11},{18,16},{19,... | collective-permute-start | bytes 786440 | tf_op jit(solution)/shard_map/ppermute | solution.py:268
  147.1 66.4 %collective-permute-start.33 = (bf16[64,2048]{1,0:T(8,128)(2,1)}, bf16[64,2048]{1,0:T(8,128)(2,1)}, u32[]{:S(2)}, u32[]{:S(2)}) collective-permute-start(bf16[64,2048]{1,0:T(8,128)(2,1)} %collective-permute-done.32), channel_id=1, source_target_pairs={{4,6},{5,7},{12,14},{13,15},{20,22},{21,23},{28,30},{29,31}} | collective-permute-start | bytes 786440 | tf_op jit(solution)/shard_map/ppermute | solution.py:268
  148.5 25.0 %collective-permute-start.15 = (f32[2,1056]{1,0:T(2,128)S(1)}, f32[2,1056]{1,0:T(2,128)S(1)}, u32[]{:S(2)}, u32[]{:S(2)}) collective-permute-start(f32[2,1056]{1,0:T(2,128)S(1)} %bitcast_add_fusion), channel_id=1, source_target_pairs={{0,4},{1,5},{2,6},{3,7},{4,0},{5,1},{6,2},{7,3},{8,12},{9,13},{10,... | collective-permute-start | bytes 25352 | tf_op jit(solution)/shard_map/ppermute | solution.py:268
  168.6 46.8 %collective-permute-start.31 = (bf16[64,2048]{1,0:T(8,128)(2,1)}, bf16[64,2048]{1,0:T(8,128)(2,1)}, u32[]{:S(2)}, u32[]{:S(2)}) collective-permute-start(bf16[64,2048]{1,0:T(8,128)(2,1)} %collective-permute-done.30), channel_id=1, source_target_pairs={{2,0},{3,1},{10,8},{11,9},{18,16},{19,17},{26,24},{27,25}} | collective-permute-start | bytes 786440 | tf_op jit(solution)/shard_map/ppermute | solution.py:268
  192.1 48.7 %collective-permute-start.56 = (bf16[32,2048]{1,0:T(8,128)(2,1)}, bf16[32,2048]{1,0:T(8,128)(2,1)}, u32[]{:S(2)}, u32[]{:S(2)}) collective-permute-start(bf16[32,2048]{1,0:T(8,128)(2,1)} %reshape.585), channel_id=1, source_target_pairs={{0,8},{8,0},{16,24},{24,16},{1,9},{9,1},{17,25},{25,17},{2,10},{10... | collective-permute-start | bytes 393224 | tf_op jit(solution)/shard_map/ppermute | solution.py:310
  194.8 53.7 %collective-permute-start.19 = (bf16[2,8,64,256]{3,2,1,0:T(8,128)(2,1)}, bf16[2,8,64,256]{3,2,1,0:T(8,128)(2,1)}, u32[]{:S(2)}, u32[]{:S(2)}) collective-permute-start(bf16[2,8,64,256]{3,2,1,0:T(8,128)(2,1)} %bitcast.21.refs_0_), channel_id=1, source_target_pairs={{0,2},{1,3},{2,4},{3,5},{4,6},{5,7},{8,10},{9,11},{10,12},{11,13},... | collective-permute-start | bytes 1572872 | tf_op jit(solution)/shard_map/ppermute | solution.py:268
  221.0 37.1 %collective-permute-start.20 = (bf16[2,8,64,256]{3,2,1,0:T(8,128)(2,1)}, bf16[2,8,64,256]{3,2,1,0:T(8,128)(2,1)}, u32[]{:S(2)}, u32[]{:S(2)}) collective-permute-start(bf16[2,8,64,256]{3,2,1,0:T(8,128)(2,1)} %bitcast.21.refs_0_), channel_id=1, source_target_pairs={{2,0},{3,1},{4,2},{5,3},{6,4},{7,5},{10,8},{11,9},{12,10},{13,11},... | collective-permute-start | bytes 1572872 | tf_op jit(solution)/shard_map/ppermute | solution.py:268
  233.7 16.2 %collective-permute-start.34 = (bf16[4,64,1024]{2,1,0:T(8,128)(2,1)}, bf16[4,64,1024]{2,1,0:T(8,128)(2,1)}, u32[]{:S(2)}, u32[]{:S(2)}) collective-permute-start(bf16[4,64,1024]{2,1,0:T(8,128)(2,1)} %get-tuple-element.79), channel_id=1, source_target_pairs={{0,8},{8,0},{16,24},{24,16},{1,9},{9,1},{17,25},{25,17},{2,10},{10... | collective-permute-start | bytes 1572872 | tf_op jit(solution)/shard_map/ppermute | solution.py:687
  240.8 14.9 %collective-permute-start.36 = (bf16[4,64,1024]{2,1,0:T(8,128)(2,1)S(1)}, bf16[4,64,1024]{2,1,0:T(8,128)(2,1)S(1)}, u32[]{:S(2)}, u32[]{:S(2)}) collective-permute-start(bf16[4,64,1024]{2,1,0:T(8,128)(2,1)S(1)} %copy-done.19), channel_id=1, source_target_pairs={{0,16},{8,24},{16,0},{24,8},{1,17},{9,25},{17,1},{25,9},{2,18},{10... | collective-permute-start | bytes 1572872 | tf_op jit(solution)/shard_map/ppermute | solution.py:688
  248.5 14.1 %collective-permute-start.18 = (bf16[2,8,64,256]{3,2,1,0:T(8,128)(2,1)}, bf16[2,8,64,256]{3,2,1,0:T(8,128)(2,1)}, u32[]{:S(2)}, u32[]{:S(2)}) collective-permute-start(bf16[2,8,64,256]{3,2,1,0:T(8,128)(2,1)} %bitcast.21.refs_0_), channel_id=1, source_target_pairs={{0,1},{1,0},{2,3},{3,2},{4,5},{5,4},{6,7},{7,6},{8,9},{9,8},{10,11... | collective-permute-start | bytes 1572872 | tf_op jit(solution)/shard_map/ppermute | solution.py:268
  248.5 14.2 %collective-permute-start.24 = (bf16[2,8,64,256]{3,2,1,0:T(8,128)(2,1)}, bf16[2,8,64,256]{3,2,1,0:T(8,128)(2,1)}, u32[]{:S(2)}, u32[]{:S(2)}) collective-permute-start(bf16[2,8,64,256]{3,2,1,0:T(8,128)(2,1)} %collective-permute-done.19), channel_id=1, source_target_pairs={{2,4},{3,5},{4,6},{5,7},{10,12},{11,13},{12,14},{13,15},{18,20},{1... | collective-permute-start | bytes 1572872 | tf_op jit(solution)/shard_map/ppermute | solution.py:268
  249.9 11.2 %collective-permute-start.57 = (bf16[2,32,2048]{2,1,0:T(8,128)(2,1)S(1)}, bf16[2,32,2048]{2,1,0:T(8,128)(2,1)S(1)}, u32[]{:S(2)}, u32[]{:S(2)}) collective-permute-start(bf16[2,32,2048]{2,1,0:T(8,128)(2,1)S(1)} %pad_maximum_fusion.12), channel_id=1, source_target_pairs={{0,16},{8,24},{16,0},{24,8},{1,17},{9,25},{17,1},{25,9},{2,18},{10... | collective-permute-start | bytes 786440 | tf_op jit(solution)/shard_map/ppermute | solution.py:311
  258.1 13.7 %collective-permute-start.21 = (bf16[2,8,64,256]{3,2,1,0:T(8,128)(2,1)}, bf16[2,8,64,256]{3,2,1,0:T(8,128)(2,1)}, u32[]{:S(2)}, u32[]{:S(2)}) collective-permute-start(bf16[2,8,64,256]{3,2,1,0:T(8,128)(2,1)} %collective-permute-done.20), channel_id=1, source_target_pairs={{2,0},{3,1},{4,2},{5,3},{10,8},{11,9},{12,10},{13,11},{18,16},{19,... | collective-permute-start | bytes 1572872 | tf_op jit(solution)/shard_map/ppermute | solution.py:268
  259.6 24.8 %collective-permute-start.35 = (bf16[2,4,64,1024]{3,2,1,0:T(8,128)(2,1)S(1)}, bf16[2,4,64,1024]{3,2,1,0:T(8,128)(2,1)}, u32[]{:S(2)}, u32[]{:S(2)}) collective-permute-start(bf16[2,4,64,1024]{3,2,1,0:T(8,128)(2,1)S(1)} %pad_maximum_fusion.4.refs_8_), channel_id=1, source_target_pairs={{0,16},{8,24},{16,0},{24,8},{1,17},{9,25},{17,1},{25,9},{2,18},{10... | collective-permute-start | bytes 3145736 | tf_op jit(solution)/shard_map/ppermute | solution.py:688
  261.1 23.8 %collective-permute-start.37 = (bf16[2,4,64,1024]{3,2,1,0:T(8,128)(2,1)}, bf16[2,4,64,1024]{3,2,1,0:T(8,128)(2,1)}, u32[]{:S(2)}, u32[]{:S(2)}) collective-permute-start(bf16[2,4,64,1024]{3,2,1,0:T(8,128)(2,1)} %pad_maximum_fusion.5.refs_10_), channel_id=1, source_target_pairs={{0,8},{8,0},{16,24},{24,16},{1,9},{9,1},{17,25},{25,17},{2,10},{10... | collective-permute-start | bytes 3145736 | tf_op jit(solution)/shard_map/ppermute | solution.py:687
  262.6 23.8 %collective-permute-start.38 = (bf16[2,4,64,1024]{3,2,1,0:T(8,128)(2,1)S(1)}, bf16[2,4,64,1024]{3,2,1,0:T(8,128)(2,1)}, u32[]{:S(2)}, u32[]{:S(2)}) collective-permute-start(bf16[2,4,64,1024]{3,2,1,0:T(8,128)(2,1)S(1)} %pad_maximum_fusion.4.refs_8_), channel_id=1, source_target_pairs={{0,1},{1,0},{2,3},{3,2},{4,5},{5,4},{6,7},{7,6},{8,9},{9,8},{10,11... | collective-permute-start | bytes 3145736 | tf_op jit(solution)/shard_map/ppermute | solution.py:268
  262.7 11.5 %collective-permute-start.26 = (bf16[2,8,64,256]{3,2,1,0:T(8,128)(2,1)}, bf16[2,8,64,256]{3,2,1,0:T(8,128)(2,1)}, u32[]{:S(2)}, u32[]{:S(2)}) collective-permute-start(bf16[2,8,64,256]{3,2,1,0:T(8,128)(2,1)} %collective-permute-done.24), channel_id=1, source_target_pairs={{4,6},{5,7},{12,14},{13,15},{20,22},{21,23},{28,30},{29,31}} | collective-permute-start | bytes 1572872 | tf_op jit(solution)/shard_map/ppermute | solution.py:268
  271.8 12.6 %collective-permute-start.22 = (bf16[2,8,64,256]{3,2,1,0:T(8,128)(2,1)}, bf16[2,8,64,256]{3,2,1,0:T(8,128)(2,1)S(1)}, u32[]{:S(2)}, u32[]{:S(2)}) collective-permute-start(bf16[2,8,64,256]{3,2,1,0:T(8,128)(2,1)} %collective-permute-done.21), channel_id=1, source_target_pairs={{2,0},{3,1},{10,8},{11,9},{18,16},{19,17},{26,24},{27,25}} | collective-permute-start | bytes 1572872 | tf_op jit(solution)/shard_map/ppermute | solution.py:268
  274.2 11.7 %collective-permute-start.25 = (bf16[2,8,64,256]{3,2,1,0:T(8,128)(2,1)S(1)}, bf16[2,8,64,256]{3,2,1,0:T(8,128)(2,1)S(1)}, u32[]{:S(2)}, u32[]{:S(2)}) collective-permute-start(bf16[2,8,64,256]{3,2,1,0:T(8,128)(2,1)S(1)} %broadcast_select_fusion.6.refs_4_), channel_id=1, source_target_pairs={{0,1},{1,0},{2,3},{3,2},{4,5},{5,4},{6,7},{7,6},{8,9},{9,8},{10,11... | collective-permute-start | bytes 1572872 | tf_op jit(solution)/shard_map/ppermute | solution.py:268
  323.8 12.8 %collective-permute-start.61 = (bf16[132,2048]{1,0:T(8,128)(2,1)}, bf16[132,2048]{1,0:T(8,128)(2,1)S(1)}, u32[]{:S(2)}, u32[]{:S(2)}) collective-permute-start(bf16[132,2048]{1,0:T(8,128)(2,1)} %get-tuple-element.52), channel_id=1, source_target_pairs={{0,1},{1,0},{2,3},{3,2},{4,5},{5,4},{6,7},{7,6},{8,9},{9,8},{10,11... | collective-permute-start | bytes 1622024 | tf_op jit(solution)/shard_map/ppermute | solution.py:268
  325.6 23.2 %collective-permute-start.67 = (bf16[4,2,132,256]{3,1,2,0:T(2,128)(2,1)S(1)}, bf16[4,2,132,256]{3,1,2,0:T(2,128)(2,1)S(1)}, u32[]{:S(2)}, u32[]{:S(2)}) collective-permute-start(bf16[4,2,132,256]{3,1,2,0:T(2,128)(2,1)S(1)} %get-tuple-element.75), channel_id=1, source_target_pairs={{0,1},{1,0},{2,3},{3,2},{4,5},{5,4},{6,7},{7,6},{8,9},{9,8},{10,11... | collective-permute-start | bytes 1622024 | tf_op jit(solution)/shard_map/ppermute | solution.py:268
  336.4 16.1 %collective-permute-start.59 = (bf16[132,2048]{1,0:T(8,128)(2,1)}, bf16[132,2048]{1,0:T(8,128)(2,1)S(1)}, u32[]{:S(2)}, u32[]{:S(2)}) collective-permute-start(bf16[132,2048]{1,0:T(8,128)(2,1)} %get-tuple-element.48), channel_id=1, source_target_pairs={{0,1},{1,0},{2,3},{3,2},{4,5},{5,4},{6,7},{7,6},{8,9},{9,8},{10,11... | collective-permute-start | bytes 1622024 | tf_op jit(solution)/shard_map/ppermute | solution.py:268
  336.7 16.4 %collective-permute-start.62 = (bf16[132,2048]{1,0:T(8,128)(2,1)S(1)}, bf16[132,2048]{1,0:T(8,128)(2,1)S(1)}, u32[]{:S(2)}, u32[]{:S(2)}) collective-permute-start(bf16[132,2048]{1,0:T(8,128)(2,1)S(1)} %add_convert_fusion.3), channel_id=1, source_target_pairs={{0,2},{1,3},{6,4},{7,5},{8,10},{9,11},{14,12},{15,13},{16,18},{17,... | collective-permute-start | bytes 1622024 | tf_op jit(solution)/shard_map/ppermute | solution.py:268
  348.5 34.7 %collective-permute-start.60 = (bf16[132,2048]{1,0:T(8,128)(2,1)}, bf16[132,2048]{1,0:T(8,128)(2,1)}, u32[]{:S(2)}, u32[]{:S(2)}) collective-permute-start(bf16[132,2048]{1,0:T(8,128)(2,1)} %get-tuple-element.50), channel_id=1, source_target_pairs={{0,1},{1,0},{2,3},{3,2},{4,5},{5,4},{6,7},{7,6},{8,9},{9,8},{10,11... | collective-permute-start | bytes 1622024 | tf_op jit(solution)/shard_map/ppermute | solution.py:268
  350.4 16.2 %collective-permute-start.70 = (bf16[2,2,132,256]{3,1,2,0:T(2,128)(2,1)S(1)}, bf16[2,2,132,256]{3,1,2,0:T(2,128)(2,1)S(1)}, u32[]{:S(2)}, u32[]{:S(2)}) collective-permute-start(bf16[2,2,132,256]{3,1,2,0:T(2,128)(2,1)S(1)} %get-tuple-element.73), channel_id=1, source_target_pairs={{0,6},{1,7},{2,0},{3,1},{4,2},{5,3},{6,4},{7,5},{8,14},{9,15},{10,... | collective-permute-start | bytes 811016 | tf_op jit(solution)/shard_map/ppermute | solution.py:268
  352.5 25.9 %collective-permute-start.68 = (bf16[2,2,132,256]{3,1,2,0:T(2,128)(2,1)S(1)}, bf16[2,2,132,256]{3,1,2,0:T(2,128)(2,1)S(1)}, u32[]{:S(2)}, u32[]{:S(2)}) collective-permute-start(bf16[2,2,132,256]{3,1,2,0:T(2,128)(2,1)S(1)} %get-tuple-element.71), channel_id=1, source_target_pairs={{0,2},{1,3},{2,4},{3,5},{4,6},{5,7},{6,0},{7,1},{8,10},{9,11},{10,... | collective-permute-start | bytes 811016 | tf_op jit(solution)/shard_map/ppermute | solution.py:268
  352.5 25.8 %collective-permute-start.69 = (bf16[2,2,132,256]{3,1,2,0:T(2,128)(2,1)S(1)}, bf16[2,2,132,256]{3,1,2,0:T(2,128)(2,1)S(1)}, u32[]{:S(2)}, u32[]{:S(2)}) collective-permute-start(bf16[2,2,132,256]{3,1,2,0:T(2,128)(2,1)S(1)} %get-tuple-element.72), channel_id=1, source_target_pairs={{0,4},{1,5},{2,6},{3,7},{4,0},{5,1},{6,2},{7,3},{8,12},{9,13},{10,... | collective-permute-start | bytes 811016 | tf_op jit(solution)/shard_map/ppermute | solution.py:268
  354.3 29.0 %collective-permute-start.63 = (bf16[132,2048]{1,0:T(8,128)(2,1)}, bf16[132,2048]{1,0:T(8,128)(2,1)}, u32[]{:S(2)}, u32[]{:S(2)}) collective-permute-start(bf16[132,2048]{1,0:T(8,128)(2,1)} %add_convert_fusion.2), channel_id=1, source_target_pairs={{0,2},{1,3},{2,4},{3,5},{8,10},{9,11},{10,12},{11,13},{16,18},{17,... | collective-permute-start | bytes 1622024 | tf_op jit(solution)/shard_map/ppermute | solution.py:268
  366.6 16.6 %collective-permute-start.65 = (bf16[132,2048]{1,0:T(8,128)(2,1)}, bf16[132,2048]{1,0:T(8,128)(2,1)}, u32[]{:S(2)}, u32[]{:S(2)}) collective-permute-start(bf16[132,2048]{1,0:T(8,128)(2,1)} %add_convert_fusion.2), channel_id=1, source_target_pairs={{4,2},{5,3},{6,4},{7,5},{12,10},{13,11},{14,12},{15,13},{20,18},{2... | collective-permute-start | bytes 1622024 | tf_op jit(solution)/shard_map/ppermute | solution.py:268
  378.3 21.0 %collective-permute-start.58 = (bf16[132,2048]{1,0:T(8,128)(2,1)}, bf16[132,2048]{1,0:T(8,128)(2,1)}, u32[]{:S(2)}, u32[]{:S(2)}) collective-permute-start(bf16[132,2048]{1,0:T(8,128)(2,1)} %get-tuple-element.46), channel_id=1, source_target_pairs={{0,1},{1,0},{2,3},{3,2},{4,5},{5,4},{6,7},{7,6},{8,9},{9,8},{10,11... | collective-permute-start | bytes 1622024 | tf_op jit(solution)/shard_map/ppermute | solution.py:268
  386.6 18.6 %collective-permute-start.64 = (bf16[132,2048]{1,0:T(8,128)(2,1)}, bf16[132,2048]{1,0:T(8,128)(2,1)S(1)}, u32[]{:S(2)}, u32[]{:S(2)}) collective-permute-start(bf16[132,2048]{1,0:T(8,128)(2,1)} %get-tuple-element.65), channel_id=1, source_target_pairs={{0,2},{1,3},{2,4},{3,5},{4,6},{5,7},{8,10},{9,11},{10,12},{11,13},... | collective-permute-start | bytes 1622024 | tf_op jit(solution)/shard_map/ppermute | solution.py:268
  393.4 16.6 %collective-permute-start.66 = (bf16[132,2048]{1,0:T(8,128)(2,1)}, bf16[132,2048]{1,0:T(8,128)(2,1)}, u32[]{:S(2)}, u32[]{:S(2)}) collective-permute-start(bf16[132,2048]{1,0:T(8,128)(2,1)} %get-tuple-element.66), channel_id=1, source_target_pairs={{2,0},{3,1},{4,2},{5,3},{6,4},{7,5},{10,8},{11,9},{12,10},{13,11},... | collective-permute-start | bytes 1622024 | tf_op jit(solution)/shard_map/ppermute | solution.py:268
  (75 other events, 718.9 us)
